TPU v7x, 32 devices: a whole 2x2x4 slice. The times are simulated.
32 devices in a mesh: space: 4 (over z), block: 8 (over y, x, core).
Axes of the slice: x: 2, y: 2, z: 4, core: 2. Of those that a mesh axis runs over, the one named last changes fastest.
Arguments:
- start_vectors: float32 [256, 16, 9216], P('block', 'space'), may hold values from -210 to 210, as said below
- phase_labels: int32 [16, 9216], P('space'), may hold values from 0 to 2
- phase_conductivity: float32 [3], replicated, may hold values from 0.3 to 3
Outputs:
- basis: float32 [256, 16, 9216], P('block', 'space')
Inputs may be any that keep to these rules, and one draw needn't show every extreme that they name: `start_vectors`: Real-valued starting vectors.
All inputs are finite; a program needn't handle non-finite values.
Results may differ from a plain program's by a relative error of at most 0.0003.
Values sent between devices are 32-bit elements; how exact they have to be, the bound alone decides.
No kernel may reach another device: no remote copies, remote signals or barrier semaphores. Data moves between devices by JAX's collectives and lax.ppermute only.
A program may use at most 128 MiB of HBM per device.

v0:
```python
import functools
import math

import jax
import jax.numpy as jnp
from jax import lax
from jax.experimental import pallas as pl
from jax.experimental.pallas import tpu as pltpu
from jax.sharding import PartitionSpec as P

NZ = 96
DEGREE = 4
LANES = 128
CHUNK = 8
PANEL = 32
HIGHEST = lax.Precision.HIGHEST


def neighbours(axis):
    count = lax.axis_size(axis)
    up = [(i, i + 1) for i in range(count - 1)]
    return up, [(b, a) for a, b in up]


def lookup(labels, table):
    return jnp.where(labels == 0, table[0], jnp.where(labels == 1, table[1], table[2]))


def face(left_k, right_k):
    filled = jnp.where(right_k > 0, right_k, left_k)
    return 2.0 * left_k * filled / (left_k + filled)


def terms_kernel(planes, scales, low, own, high, out, window):
    scale, shift = scales[0], scales[1]
    count = out.shape[0]
    window[...] = jnp.zeros_like(window)
    for k, source in enumerate((low, own, high)):
        window[k * planes : (k + 1) * planes, :] = source[0]
    cells = window.shape[1]
    span = 3 * LANES * NZ // math.gcd(3 * LANES, NZ)
    assert cells % span == 0
    z = lax.rem(lax.broadcasted_iota(jnp.int32, (8, span), 1), NZ)

    def body(g, carry):
        lanes = pl.ds(pl.multiple_of(g * span, span), span)
        left = pl.ds(pl.multiple_of(jnp.maximum(g * span - LANES, 0), LANES), LANES)
        right = pl.ds(
            pl.multiple_of(jnp.minimum(g * span + span, cells - LANES), LANES), LANES
        )
        for base in range(0, count, 8):
            rows = pl.ds(base + 1, 8)
            kappa = window[rows, lanes]
            inside = kappa > 0
            safe = jnp.where(inside, kappa, 1.0)
            before = jnp.where(g == 0, 0.0, window[rows, left])
            after = jnp.where(g * span + span == cells, 0.0, window[rows, right])
            wide = jnp.concatenate([before, kappa, after], axis=1)
            total = wide.shape[1]

            def moved(offset):
                return pltpu.roll(wide, (-offset) % total, 1)[:, LANES : LANES + span]

            around = [
                window[pl.ds(base, 8), lanes],
                window[pl.ds(base + 2, 8), lanes],
                jnp.where(z < NZ - 1, moved(1), 0.0),
                jnp.where(z > 0, moved(-1), 0.0),
                moved(NZ),
                moved(-NZ),
            ]
            faces = [face(safe, k) for k in around]
            diagonal = functools.reduce(jnp.add, faces) - shift
            values = [jnp.where(inside, diagonal * scale, 0.0)]
            for f, k in zip(faces, around):
                values.append(jnp.where(inside & (k > 0), -scale * f, 0.0))
            kept = min(8, count - base)
            for k, value in enumerate(values):
                out[base : base + kept, k, lanes] = value[:kept]
        return carry

    lax.fori_loop(0, cells // span, body, 0)


def stencil_terms(low, own, high, centre, radius):
    planes, cells = own.shape[1:]
    inner = 3 * planes - 2
    smem, vmem = pl.BlockSpec(memory_space=pltpu.SMEM), pl.BlockSpec(memory_space=pltpu.VMEM)
    return pl.pallas_call(
        functools.partial(terms_kernel, planes),
        out_shape=jax.ShapeDtypeStruct((inner, 8, cells), jnp.float32),
        in_specs=[smem] + [vmem] * 3,
        out_specs=vmem,
        scratch_shapes=[pltpu.VMEM((24, cells), jnp.float32)],
        compiler_params=pltpu.CompilerParams(vmem_limit_bytes=24 * 2**20),
        name="stencil_terms",
    )(jnp.stack([2.0 / radius, centre]), low, own, high)


def filter_kernel(planes, halves, low, own, high, terms, out, y0, y1, y2, y3):
    for k, source in enumerate((low, own, high)):
        for p in range(planes):
            y0[k * planes + p] = source[0:CHUNK, p, :]
    cells = y0.shape[-1]
    tiles = cells // LANES
    per_half = tiles // halves
    group = per_half
    lane = lax.broadcasted_iota(jnp.int32, (CHUNK, LANES), 1)
    last, first = lane == LANES - 1, lane == 0
    head, tail = lane < NZ, lane >= LANES - NZ

    def sweep(source, source_at, previous, previous_at, target, at, half_step):
        count = target_planes(target)

        def plane_body(p, carry):
            w = p + at

            def group_body(g, carry):
                t0 = g * group
                s = source_at(w)
                span = pl.ds(pl.multiple_of(t0 * LANES, LANES), group * LANES)
                before = jnp.where(t0 == 0, tiles - 1, t0 - 1)
                after = jnp.where(t0 + group == tiles, 0, t0 + group)

                def edge(t):
                    return source[s, :, pl.ds(pl.multiple_of(t * LANES, LANES), LANES)]

                def cut(wide):
                    return [wide[:, i * LANES : (i + 1) * LANES] for i in range(group)]

                row = [edge(before)] + cut(source[s, :, span]) + [edge(after)]
                below, above = cut(source[s - 1, :, span]), cut(source[s + 1, :, span])
                rows = [cut(terms[w - 1, pl.ds(k, 1), span]) for k in range(7)]
                if not half_step:
                    older = cut(previous[previous_at(w), :, span])
                results = []
                for i in range(group):
                    left, here, right = row[i : i + 3]
                    total = rows[0][i] * here
                    total += rows[1][i] * below[i]
                    total += rows[2][i] * above[i]
                    total += rows[3][i] * pltpu.roll(jnp.where(first, right, here), LANES - 1, 1)
                    total += rows[4][i] * pltpu.roll(jnp.where(last, left, here), 1, 1)
                    total += rows[5][i] * pltpu.roll(jnp.where(head, right, here), LANES - NZ, 1)
                    total += rows[6][i] * pltpu.roll(jnp.where(tail, left, here), NZ, 1)
                    results.append(0.5 * total if half_step else total - older[i])
                result = jnp.concatenate(results, axis=1)
                if target is out:
                    half = lax.div(t0, per_half)
                    inner = pl.multiple_of((t0 - half * per_half) * LANES, LANES)
                    out[p * halves + half, :, pl.ds(inner, group * LANES)] = result
                else:
                    target[p, :, span] = result
                return carry

            return lax.fori_loop(0, tiles // group, group_body, carry, unroll=True)

        lax.fori_loop(0, count, plane_body, 0)

    def target_planes(target):
        return planes if target is out else target.shape[0]

    sweep(y0, lambda w: w, None, None, y1, 1, True)
    sweep(y1, lambda w: w - 1, y0, lambda w: w, y2, 2, False)
    sweep(y2, lambda w: w - 2, y1, lambda w: w - 1, y3, 3, False)
    sweep(y3, lambda w: w - 3, y2, lambda w: w - 2, out, 4, False)


def filtered(low, own, high, terms, blocks):
    planes, cells = own.shape[1:]
    halves = blocks // planes
    width = cells // halves
    steps = (3 * planes, 3 * planes - 2, 3 * planes - 4, 3 * planes - 6)
    vmem = pl.BlockSpec(memory_space=pltpu.VMEM)
    return pl.pallas_call(
        functools.partial(filter_kernel, planes, halves),
        out_shape=jax.ShapeDtypeStruct((blocks, CHUNK, width), jnp.float32),
        in_specs=[vmem] * 4,
        out_specs=vmem,
        scratch_shapes=[pltpu.VMEM((count, CHUNK, cells), jnp.float32) for count in steps],
        compiler_params=pltpu.CompilerParams(vmem_limit_bytes=32 * 2**20),
        cost_estimate=pl.CostEstimate(
            flops=14 * 7 * planes * CHUNK * cells,
            bytes_accessed=4 * 44 * CHUNK * cells,
            transcendentals=0,
        ),
        name="chebyshev",
    )(low, own, high, terms)


def assemble_kernel(planes, source, out):
    for m in range(0, out.shape[0], 8):
        for p in range(planes):
            out[m : m + 8, p, :] = source[p, 0, m : m + 8, :]


def assembled(pieces):
    planes, halves, rows, width = pieces.shape
    return pl.pallas_call(
        functools.partial(assemble_kernel, planes),
        grid=(halves,),
        out_shape=jax.ShapeDtypeStruct((rows, planes, halves * width), jnp.float32),
        in_specs=[pl.BlockSpec((planes, 1, rows, width), lambda i: (0, i, 0, 0))],
        out_specs=pl.BlockSpec((rows, planes, width), lambda i: (0, 0, i)),
        compiler_params=pltpu.CompilerParams(vmem_limit_bytes=32 * 2**20),
        name="assemble",
    )(pieces)


def inverse_factor_kernel(scale, gram, out, work):
    rank = gram.shape[0]
    work[...] = gram[...] * scale
    lane = lax.broadcasted_iota(jnp.int32, (8, rank), 1)
    sub = lax.broadcasted_iota(jnp.int32, (8, 1), 0)
    for k0 in range(0, rank, PANEL):
        groups = [work[k0 + 8 * g : k0 + 8 * g + 8, :] for g in range(PANEL // 8)]
        pivots = [jnp.ones((8, 1), jnp.float32)] * len(groups)
        for j in range(PANEL):
            at, inner, column = j // 8, j % 8, k0 + j
            here = lane == column
            pivot = groups[at][inner : inner + 1, column : column + 1]
            inverse = 1.0 / pivot
            pivots[at] = jnp.where(sub == inner, pivot, pivots[at])
            row = jnp.where(here[:1], 1.0, groups[at][inner : inner + 1, :]) * inverse
            for g in range(at, len(groups)):
                factor = groups[g][:, column : column + 1]
                if g == at:
                    factor = jnp.where(sub > inner, factor, 0.0)
                    kept = jnp.where(here, jnp.where(sub == inner, 1.0, 0.0), groups[g])
                    if inner:
                        kept = jnp.where(sub < inner, groups[g], kept)
                else:
                    kept = jnp.where(here, 0.0, groups[g])
                groups[g] = kept - factor * row
        scaled = [v / jnp.sqrt(p) for v, p in zip(groups, pivots)]
        panel = jnp.concatenate(scaled, axis=0)
        done = k0 + PANEL
        columns = lax.broadcasted_iota(jnp.int32, (PANEL, rank), 1)
        rows = k0 + lax.broadcasted_iota(jnp.int32, (PANEL, rank), 0)
        behind = columns <= rows
        out[k0:done, :] = jnp.where(behind, panel, 0.0)
        panel = jnp.where(behind | (columns >= done), panel, 0.0)
        if done < rank:
            update = lax.dot_general(
                panel, panel, (((0,), (0,)), ((), ())), precision=HIGHEST,
                preferred_element_type=jnp.float32,
            )
            inside = (columns[:1] >= k0) & (columns[:1] < done)
            work[done:, :] = jnp.where(inside, 0.0, work[done:, :]) - update[done:, :]


def inverse_factor(gram, scale):
    rank = gram.shape[0]
    return pl.pallas_call(
        functools.partial(inverse_factor_kernel, scale),
        out_shape=jax.ShapeDtypeStruct((rank, rank), jnp.float32),
        in_specs=[pl.BlockSpec(memory_space=pltpu.VMEM)],
        out_specs=pl.BlockSpec(memory_space=pltpu.VMEM),
        scratch_shapes=[pltpu.VMEM((rank, rank), jnp.float32)],
        name="inverse_factor",
    )(gram)


def local(start_vectors, phase_labels, phase_conductivity):
    upper_bound = 12.0 * jnp.max(phase_conductivity)
    lower_bound = upper_bound / 10.0
    centre = (upper_bound + lower_bound) / 2.0
    radius = (upper_bound - lower_bound) / 2.0
    per_device, planes, plane_cells = start_vectors.shape
    blocks, slabs = lax.axis_size("block"), lax.axis_size("space")
    assert planes == DEGREE and blocks % planes == 0
    halves = blocks // planes
    width = plane_cells // halves
    cells = planes * slabs * plane_cells
    rank = per_device * blocks
    up, back = neighbours("space")
    chunks = per_device // CHUNK

    conduct = lookup(phase_labels, phase_conductivity)
    received = []
    for c in range(chunks):
        own = start_vectors[c * CHUNK : (c + 1) * CHUNK]
        if c == 0:
            own = jnp.concatenate([own, conduct[None]], axis=0)
        low = lax.ppermute(own, "space", up)
        high = lax.ppermute(own, "space", back)
        if c == 0:
            terms = stencil_terms(
                low[CHUNK:], conduct[None], high[CHUNK:], centre, radius
            )
        part = filtered(low, own, high, terms, blocks)
        received.append(lax.all_to_all(part, "block", 0, 0, tiled=True))
    field = jnp.stack(received, axis=1).reshape(rank, width)

    partial = jnp.einsum("mp,np->mn", field, field, precision=HIGHEST)
    devices = blocks * slabs
    pieces = partial.reshape(devices, rank // devices, rank)
    summed = jnp.sum(lax.all_to_all(pieces, ("space", "block"), 0, 0, tiled=True), axis=0)
    gram = lax.all_to_all(
        jnp.broadcast_to(summed[None], pieces.shape), ("space", "block"), 0, 0, tiled=True
    ).reshape(rank, rank)
    inverse = inverse_factor(gram, 1.0 / cells)
    result = jnp.einsum("mn,np->mp", inverse, field, precision=HIGHEST)
    sent = lax.all_to_all(result.reshape(blocks, per_device, width), "block", 0, 0, tiled=True)
    return assembled(sent.reshape(planes, halves, per_device, width))


def solution(mesh):
    return jax.shard_map(
        local,
        mesh=mesh,
        in_specs=(P("block", "space", None), P("space", None), P()),
        out_specs=P("block", "space", None),
        check_vma=False,
    )
```

profile of v0, /device:TPU:0, one launch (start us, length us, event | category | flops | bytes accessed | tf_op | source)
XLA Modules:
  0.0 291.2 jit_solution(12013758431668926193)
XLA Ops:
  1.4 4.4 %fusion = (f32[8,4,9216]{2,1,0:T(4,128)}, f32[8,4,9216]{2,1,0:T(4,128)S(1)}, f32[8,4,9216]{2,1,0:T(4,128)}, f32[8,4,9216]{2,1,0:T(4,128)}) fusion(f32[32,4,9216]{2,1,0:T(4,128)} %param.3), kind=kLoop, calls=%fused_computation.4 | loop fusion | bytes 9437184 | tf_op jit(solution)/shard_map/slice | solution.py:282
  8.1 5.0 %collective-permute-start = (f32[9,4,9216]{2,1,0:T(4,128)S(1)}, f32[9,4,9216]{2,1,0:T(4,128)S(1)}, u32[]{:S(2)}, u32[]{:S(2)}) collective-permute-start(f32[9,4,9216]{2,1,0:T(4,128)S(1)} %pad_maximum_fusion.1.own), channel_id=1, source_target_pairs={{0,8},{8,16},{16,24},{1,9},{9,17},{17,25},{2,10},{10,18},{18,26},{... | collective-permute-start | bytes 3981320 | tf_op jit(solution)/shard_map/ppermute | solution.py:285
  15.5 5.6 %collective-permute-start.2 = (f32[8,4,9216]{2,1,0:T(4,128)}, f32[8,4,9216]{2,1,0:T(4,128)}, u32[]{:S(2)}, u32[]{:S(2)}) collective-permute-start(f32[8,4,9216]{2,1,0:T(4,128)} %get-tuple-element.5.own), channel_id=1, source_target_pairs={{0,8},{8,16},{16,24},{1,9},{9,17},{17,25},{2,10},{10,18},{18,26},{... | collective-permute-start | bytes 3538952 | tf_op jit(solution)/shard_map/ppermute | solution.py:285
  24.4 18.1 %collective-permute-done.low = f32[9,4,9216]{2,1,0:T(4,128)S(1)} collective-permute-done((f32[9,4,9216]{2,1,0:T(4,128)S(1)}, f32[9,4,9216]{2,1,0:T(4,128)S(1)}, u32[]{:S(2)}, u32[]{:S(2)}) %collective-permute-start) | collective-permute-done | bytes 1327136 | tf_op jit(solution)/shard_map/ppermute | solution.py:285
  43.6 3.5 %collective-permute-done.1.high = f32[9,4,9216]{2,1,0:T(4,128)} collective-permute-done((f32[9,4,9216]{2,1,0:T(4,128)S(1)}, f32[9,4,9216]{2,1,0:T(4,128)}, u32[]{:S(2)}, u32[]{:S(2)}) %collective-permute-start.1) | collective-permute-done | bytes 1327136 | tf_op jit(solution)/shard_map/ppermute | solution.py:286
  48.1 5.0 %stencil_terms.1.terms = f32[10,8,9216]{2,1,0:T(8,128)S(1)} custom-call(f32[2]{0:T(128)S(1)} %pad_maximum_fusion.2.scales, f32[1,4,9216]{2,1,0:T(4,128)S(1)} %slice.36.low, f32[1,4,9216]{2,1,0:T(4,128)S(1)} %select_bitcast_fusion.own, f32[1,4,9216]{2,1,0:T(4,128)S(1)} %slice.37.high), custom_call_target="tpu_custom_call" | custom-call | tf_op jit(solution)/shard_map/stencil_terms/pallas_call | solution.py:89
  53.1 12.4 %chebyshev.4 = f32[8,8,4608]{2,1,0:T(8,128)S(1)} custom-call(f32[9,4,9216]{2,1,0:T(4,128)S(1)} %copy-done.9, f32[9,4,9216]{2,1,0:T(4,128)S(1)} %copy-done.1, f32[9,4,9216]{2,1,0:T(4,128)} %collective-permute-done.1.high, f32[10,8,9216]{2,1,0:T(8,128)S(1)} %stencil_terms.1.terms), custom_call_target="tpu_custom_call" | custom-call | flops 28901376 | bytes 12976128 | tf_op jit(solution)/shard_map/chebyshev/pallas_call | solution.py:175
  66.6 4.3 %all-to-all-start = ((f32[8,8,4608]{2,1,0:T(8,128)}), f32[8,8,4608]{2,1,0:T(8,128)}, u32[]{:S(2)}, u32[]{:S(2)}) async-start(f32[8,8,4608]{2,1,0:T(8,128)} %copy-done.4), calls=%async_computation | async-start | bytes 2359296 | tf_op jit(solution)/shard_map/all_to_all | solution.py:292
  70.9 4.5 %collective-permute-start.4 = (f32[8,4,9216]{2,1,0:T(4,128)}, f32[8,4,9216]{2,1,0:T(4,128)}, u32[]{:S(2)}, u32[]{:S(2)}) collective-permute-start(f32[8,4,9216]{2,1,0:T(4,128)} %get-tuple-element.8.own), channel_id=1, source_target_pairs={{0,8},{8,16},{16,24},{1,9},{9,17},{17,25},{2,10},{10,18},{18,26},{... | collective-permute-start | bytes 3538952 | tf_op jit(solution)/shard_map/ppermute | solution.py:285
  76.6 13.1 %chebyshev.5 = f32[8,8,4608]{2,1,0:T(8,128)S(1)} custom-call(f32[8,4,9216]{2,1,0:T(4,128)} %collective-permute-done.2.low, f32[8,4,9216]{2,1,0:T(4,128)} %get-tuple-element.5.own, f32[8,4,9216]{2,1,0:T(4,128)} %collective-permute-done.3.high, f32[10,8,9216]{2,1,0:T(8,128)S(1)} %stencil_terms.1.terms), custom_call_target="tpu_custom_call" | custom-call | flops 28901376 | bytes 12976128 | tf_op jit(solution)/shard_map/chebyshev/pallas_call | solution.py:175
  90.7 4.2 %all-to-all-start.1 = ((f32[8,8,4608]{2,1,0:T(8,128)}), f32[8,8,4608]{2,1,0:T(8,128)}, u32[]{:S(2)}, u32[]{:S(2)}) async-start(f32[8,8,4608]{2,1,0:T(8,128)} %copy-done.5), calls=%async_computation.1 | async-start | bytes 2359296 | tf_op jit(solution)/shard_map/all_to_all | solution.py:292
  95.0 5.6 %collective-permute-start.6 = (f32[8,4,9216]{2,1,0:T(4,128)}, f32[8,4,9216]{2,1,0:T(4,128)}, u32[]{:S(2)}, u32[]{:S(2)}) collective-permute-start(f32[8,4,9216]{2,1,0:T(4,128)} %get-tuple-element.7.own), channel_id=1, source_target_pairs={{0,8},{8,16},{16,24},{1,9},{9,17},{17,25},{2,10},{10,18},{18,26},{... | collective-permute-start | bytes 3538952 | tf_op jit(solution)/shard_map/ppermute | solution.py:285
  101.9 3.6 %collective-permute-done.5.high = f32[8,4,9216]{2,1,0:T(4,128)} collective-permute-done((f32[8,4,9216]{2,1,0:T(4,128)}, f32[8,4,9216]{2,1,0:T(4,128)}, u32[]{:S(2)}, u32[]{:S(2)}) %collective-permute-start.5) | collective-permute-done | bytes 1179680 | tf_op jit(solution)/shard_map/ppermute | solution.py:286
  106.8 12.7 %chebyshev.6 = f32[8,8,4608]{2,1,0:T(8,128)S(1)} custom-call(f32[8,4,9216]{2,1,0:T(4,128)} %collective-permute-done.4.low, f32[8,4,9216]{2,1,0:T(4,128)S(1)} %copy-done.3, f32[8,4,9216]{2,1,0:T(4,128)} %collective-permute-done.5.high, f32[10,8,9216]{2,1,0:T(8,128)S(1)} %stencil_terms.1.terms), custom_call_target="tpu_custom_call" | custom-call | flops 28901376 | bytes 12976128 | tf_op jit(solution)/shard_map/chebyshev/pallas_call | solution.py:175
  120.5 4.2 %all-to-all-start.2 = ((f32[8,8,4608]{2,1,0:T(8,128)}), f32[8,8,4608]{2,1,0:T(8,128)}, u32[]{:S(2)}, u32[]{:S(2)}) async-start(f32[8,8,4608]{2,1,0:T(8,128)} %copy-done.6), calls=%async_computation.2 | async-start | bytes 2359296 | tf_op jit(solution)/shard_map/all_to_all | solution.py:292
  125.6 5.2 %collective-permute-done.7.high = f32[8,4,9216]{2,1,0:T(4,128)} collective-permute-done((f32[8,4,9216]{2,1,0:T(4,128)}, f32[8,4,9216]{2,1,0:T(4,128)}, u32[]{:S(2)}, u32[]{:S(2)}) %collective-permute-start.7) | collective-permute-done | bytes 1179680 | tf_op jit(solution)/shard_map/ppermute | solution.py:286
  132.0 12.7 %chebyshev.7 = f32[8,8,4608]{2,1,0:T(8,128)S(1)} custom-call(f32[8,4,9216]{2,1,0:T(4,128)} %collective-permute-done.6.low, f32[8,4,9216]{2,1,0:T(4,128)S(1)} %copy-done.2, f32[8,4,9216]{2,1,0:T(4,128)} %collective-permute-done.7.high, f32[10,8,9216]{2,1,0:T(8,128)S(1)} %stencil_terms.1.terms), custom_call_target="tpu_custom_call" | custom-call | flops 28901376 | bytes 12976128 | tf_op jit(solution)/shard_map/chebyshev/pallas_call | solution.py:175
  145.8 20.6 %all_to_all.35 = f32[8,8,4608]{2,1,0:T(8,128)S(1)} all-to-all(f32[8,8,4608]{2,1,0:T(8,128)} %copy-done.7), channel_id=1, replica_groups=mesh['space'=4,'block'=8] {'block'}, dimensions={0} | all-to-all | bytes 2359296 | tf_op jit(solution)/shard_map/all_to_all | solution.py:292
  169.1 4.0 %fusion.2 = f32[32,8,256]{2,1,0:T(8,128)S(1)} fusion(f32[32,8,4608]{2,1,0:T(8,128)S(1)} %bitcast.23, f32[256,4608,1]{1,0,2:T(8,128)S(1)} %bitcast.24), kind=kOutput, calls=%fused_computation.6 | convolution fusion | flops 3623878656 | bytes 9699328 | tf_op jit(solution)/shard_map/mp,np->mn/dot_general | solution.py:295
  173.1 12.3 %all_to_all.36 = f32[32,8,256]{2,1,0:T(8,128)S(1)} all-to-all(f32[32,8,256]{2,1,0:T(8,128)S(1)} %fusion.2), channel_id=1, replica_groups=mesh['space'=4,'block'=8] {'space','block'}, dimensions={0} | all-to-all | bytes 524288 | tf_op jit(solution)/shard_map/all_to_all | solution.py:298
  185.5 13.0 %all_to_all.37 = f32[32,8,256]{2,1,0:T(8,128)} all-to-all(f32[32,8,256]{2,1,0:T(8,128)S(1)} %broadcast_in_dim.26), channel_id=1, replica_groups=mesh['space'=4,'block'=8] {'space','block'}, dimensions={0} | all-to-all | bytes 524288 | tf_op jit(solution)/shard_map/all_to_all | solution.py:299
  198.5 26.5 %inverse_factor.1 = f32[256,256]{1,0:T(8,128)} custom-call(f32[256,256]{1,0:T(8,128)} %bitcast.28), custom_call_target="tpu_custom_call" | custom-call | tf_op jit(solution)/shard_map/inverse_factor/pallas_call | solution.py:254
  225.0 6.0 %fusion.3 = f32[8,32,4608]{2,1,0:T(8,128)S(1)} fusion(f32[8,32,256]{2,1,0:T(8,128)} %bitcast.27, f32[256,4608,1]{1,0,2:T(8,128)} %bitcast.25), kind=kOutput, calls=%fused_computation.7 | convolution fusion | flops 3623878656 | bytes 9699328 | tf_op jit(solution)/shard_map/mn,np->mp/dot_general | solution.py:303
  231.0 57.2 %all_to_all.38 = f32[8,32,4608]{2,1,0:T(8,128)S(1)} all-to-all(f32[8,32,4608]{2,1,0:T(8,128)S(1)} %fusion.3), channel_id=1, replica_groups=mesh['space'=4,'block'=8] {'block'}, dimensions={0} | all-to-all | bytes 9437184 | tf_op jit(solution)/shard_map/all_to_all | solution.py:304
  (49 shorter events, 25.8 us)
Async XLA Ops:
  1.4 4.4 %copy-start.11 = (s32[4,9216]{1,0:T(4,128)S(1)}, s32[4,9216]{1,0:T(4,128)}, u32[]{:S(2)}) copy-start(s32[4,9216]{1,0:T(4,128)} %param.4) | copy-start | bytes 442372
  7.7 14.7 %copy-start.12 = (f32[3]{0:T(128)S(1)}, f32[3]{0:T(128)}, u32[]{:S(2)}) copy-start(f32[3]{0:T(128)} %param.5) | copy-start | bytes 40
  8.1 34.5 %collective-permute-start = (f32[9,4,9216]{2,1,0:T(4,128)S(1)}, f32[9,4,9216]{2,1,0:T(4,128)S(1)}, u32[]{:S(2)}, u32[]{:S(2)}) collective-permute-start(f32[9,4,9216]{2,1,0:T(4,128)S(1)} %pad_maximum_fusion.1.own), channel_id=1, source_target_pairs={{0,8},{8,16},{16,24},{1,9},{9,17},{17,25},{2,10},{10,18},{18,26},{... | collective-permute-start | bytes 3981320 | tf_op jit(solution)/shard_map/ppermute | solution.py:285
  13.1 34.1 %collective-permute-start.1 = (f32[9,4,9216]{2,1,0:T(4,128)S(1)}, f32[9,4,9216]{2,1,0:T(4,128)}, u32[]{:S(2)}, u32[]{:S(2)}) collective-permute-start(f32[9,4,9216]{2,1,0:T(4,128)S(1)} %pad_maximum_fusion.1.own), channel_id=1, source_target_pairs={{8,0},{16,8},{24,16},{9,1},{17,9},{25,17},{10,2},{18,10},{26,18},{... | collective-permute-start | bytes 3981320 | tf_op jit(solution)/shard_map/ppermute | solution.py:286
  14.4 1.1 copy-start
  15.5 61.1 %collective-permute-start.2 = (f32[8,4,9216]{2,1,0:T(4,128)}, f32[8,4,9216]{2,1,0:T(4,128)}, u32[]{:S(2)}, u32[]{:S(2)}) collective-permute-start(f32[8,4,9216]{2,1,0:T(4,128)} %get-tuple-element.5.own), channel_id=1, source_target_pairs={{0,8},{8,16},{16,24},{1,9},{9,17},{17,25},{2,10},{10,18},{18,26},{... | collective-permute-start | bytes 3538952 | tf_op jit(solution)/shard_map/ppermute | solution.py:285
  21.1 55.5 %collective-permute-start.3 = (f32[8,4,9216]{2,1,0:T(4,128)}, f32[8,4,9216]{2,1,0:T(4,128)}, u32[]{:S(2)}, u32[]{:S(2)}) collective-permute-start(f32[8,4,9216]{2,1,0:T(4,128)} %get-tuple-element.5.own), channel_id=1, source_target_pairs={{8,0},{16,8},{24,16},{9,1},{17,9},{25,17},{10,2},{18,10},{26,18},{... | collective-permute-start | bytes 3538952 | tf_op jit(solution)/shard_map/ppermute | solution.py:286
  42.5 1.1 copy-start.8
  48.1 5.0 %copy-start.1 = (f32[9,4,9216]{2,1,0:T(4,128)S(1)}, f32[9,4,9216]{2,1,0:T(4,128)}, u32[]{:S(2)}) copy-start(f32[9,4,9216]{2,1,0:T(4,128)} %copy-done) | copy-start | bytes 3981316
  48.1 5.0 %copy-start.9 = (f32[9,4,9216]{2,1,0:T(4,128)S(1)}, f32[9,4,9216]{2,1,0:T(4,128)}, u32[]{:S(2)}) copy-start(f32[9,4,9216]{2,1,0:T(4,128)} %copy-done.8) | copy-start | bytes 3981316
  65.5 1.1 copy-start.4
  66.6 24.1 %all-to-all-start = ((f32[8,8,4608]{2,1,0:T(8,128)}), f32[8,8,4608]{2,1,0:T(8,128)}, u32[]{:S(2)}, u32[]{:S(2)}) async-start(f32[8,8,4608]{2,1,0:T(8,128)} %copy-done.4), calls=%async_computation | async-start | bytes 2359296 | tf_op jit(solution)/shard_map/all_to_all | solution.py:292
  70.9 31.0 %collective-permute-start.4 = (f32[8,4,9216]{2,1,0:T(4,128)}, f32[8,4,9216]{2,1,0:T(4,128)}, u32[]{:S(2)}, u32[]{:S(2)}) collective-permute-start(f32[8,4,9216]{2,1,0:T(4,128)} %get-tuple-element.8.own), channel_id=1, source_target_pairs={{0,8},{8,16},{16,24},{1,9},{9,17},{17,25},{2,10},{10,18},{18,26},{... | collective-permute-start | bytes 3538952 | tf_op jit(solution)/shard_map/ppermute | solution.py:285
  75.3 30.1 %collective-permute-start.5 = (f32[8,4,9216]{2,1,0:T(4,128)}, f32[8,4,9216]{2,1,0:T(4,128)}, u32[]{:S(2)}, u32[]{:S(2)}) collective-permute-start(f32[8,4,9216]{2,1,0:T(4,128)} %get-tuple-element.8.own), channel_id=1, source_target_pairs={{8,0},{16,8},{24,16},{9,1},{17,9},{25,17},{10,2},{18,10},{26,18},{... | collective-permute-start | bytes 3538952 | tf_op jit(solution)/shard_map/ppermute | solution.py:286
  89.7 1.0 copy-start.5
  90.7 29.8 %all-to-all-start.1 = ((f32[8,8,4608]{2,1,0:T(8,128)}), f32[8,8,4608]{2,1,0:T(8,128)}, u32[]{:S(2)}, u32[]{:S(2)}) async-start(f32[8,8,4608]{2,1,0:T(8,128)} %copy-done.5), calls=%async_computation.1 | async-start | bytes 2359296 | tf_op jit(solution)/shard_map/all_to_all | solution.py:292
  95.0 30.6 %collective-permute-start.6 = (f32[8,4,9216]{2,1,0:T(4,128)}, f32[8,4,9216]{2,1,0:T(4,128)}, u32[]{:S(2)}, u32[]{:S(2)}) collective-permute-start(f32[8,4,9216]{2,1,0:T(4,128)} %get-tuple-element.7.own), channel_id=1, source_target_pairs={{0,8},{8,16},{16,24},{1,9},{9,17},{17,25},{2,10},{10,18},{18,26},{... | collective-permute-start | bytes 3538952 | tf_op jit(solution)/shard_map/ppermute | solution.py:285
  100.6 30.1 %collective-permute-start.7 = (f32[8,4,9216]{2,1,0:T(4,128)}, f32[8,4,9216]{2,1,0:T(4,128)}, u32[]{:S(2)}, u32[]{:S(2)}) collective-permute-start(f32[8,4,9216]{2,1,0:T(4,128)} %get-tuple-element.7.own), channel_id=1, source_target_pairs={{8,0},{16,8},{24,16},{9,1},{17,9},{25,17},{10,2},{18,10},{26,18},{... | collective-permute-start | bytes 3538952 | tf_op jit(solution)/shard_map/ppermute | solution.py:286
  105.5 1.3 copy-start.3
  119.5 1.1 copy-start.6
  120.5 25.2 %all-to-all-start.2 = ((f32[8,8,4608]{2,1,0:T(8,128)}), f32[8,8,4608]{2,1,0:T(8,128)}, u32[]{:S(2)}, u32[]{:S(2)}) async-start(f32[8,8,4608]{2,1,0:T(8,128)} %copy-done.6), calls=%async_computation.2 | async-start | bytes 2359296 | tf_op jit(solution)/shard_map/all_to_all | solution.py:292
  130.8 1.3 copy-start.2
  144.7 1.0 copy-start.7
  169.1 4.0 %copy-start.10 = (f32[8,4,8,4608]{3,2,1,0:T(8,128)}, f32[8,4,8,4608]{3,2,1,0:T(8,128)S(1)}, u32[]{:S(2)}) copy-start(f32[8,4,8,4608]{3,2,1,0:T(8,128)S(1)} %copy.4) | copy-start | bytes 14155780
where the time goes:
time: 292 us; the launch traced here: 291 us
  blocking collectives  103 us (35%)
  Pallas kernels  85.3 us (29%)
  starting transfers between devices  38.6 us (13%)
  waiting for transfers between devices  31.2 us (11%)
  local copies, waits for them, and re-layouts  15.9 us (5%)
  matrix products  9.99 us (3%)
  other arithmetic  5.31 us (2%)
    all_to_all x1, blocking collectives, local(): lax.all_to_all(result.reshape(blocks, per_device, width), 'block', 0, 0,...  57.2 us
    pallas_call x4, Pallas kernels, filtered(): pl.pallas_call(functools.partial(filter_kernel, planes, halves), out_shap...  50.9 us
    pallas_call x1, Pallas kernels, inverse_factor(): pl.pallas_call(functools.partial(inverse_factor_kernel, scale), out_shape...  26.5 us
    ppermute x4, starting transfers between devices, local(): low = lax.ppermute(own, 'space', up)  20.7 us
    all_to_all x1, blocking collectives, local(): received.append(lax.all_to_all(part, 'block', 0, 0, tiled=True))  20.6 us
    ppermute x4, waiting for transfers between devices, local(): low = lax.ppermute(own, 'space', up)  18.9 us
    all_to_all x1, blocking collectives, local(): lax.all_to_all(jnp.broadcast_to(summed[None], pieces.shape), ('space', 'b...  13 us
    all_to_all x3, starting transfers between devices, local(): received.append(lax.all_to_all(part, 'block', 0, 0, tiled=True))  12.7 us
  transfers between devices with their start and end apart: 11, of which 5 were waited for; matrix products, arithmetic and copies ran while one was open for 1% of the time, Pallas kernels for 19%

commit v1 on v0

--- a/solution.py
+++ b/solution.py
@@ -12,7 +12,8 @@
 DEGREE = 4
 LANES = 128
 CHUNK = 8
-PANEL = 32
+PANEL = 64
+BLOCK = 9 * LANES
 HIGHEST = lax.Precision.HIGHEST
 
 
@@ -22,8 +23,26 @@
     return up, [(b, a) for a, b in up]
 
 
-def lookup(labels, table):
-    return jnp.where(labels == 0, table[0], jnp.where(labels == 1, table[1], table[2]))
+def first_chunk_kernel(table, labels, vectors, out):
+    out[0:CHUNK] = vectors[...]
+    phase = labels[...]
+    out[CHUNK] = jnp.where(phase == 0, table[0], jnp.where(phase == 1, table[1], table[2]))
+
+
+def first_chunk(vectors, labels, table):
+    planes, cells = labels.shape
+    return pl.pallas_call(
+        first_chunk_kernel,
+        grid=(1,),
+        out_shape=jax.ShapeDtypeStruct((CHUNK + 1, planes, cells), jnp.float32),
+        in_specs=[
+            pl.BlockSpec(memory_space=pltpu.SMEM),
+            pl.BlockSpec((planes, cells), lambda i: (0, 0)),
+            pl.BlockSpec((CHUNK, planes, cells), lambda i: (0, 0, 0)),
+        ],
+        out_specs=pl.BlockSpec((CHUNK + 1, planes, cells), lambda i: (0, 0, 0)),
+        name="first_chunk",
+    )(table, labels, vectors)
 
 
 def face(left_k, right_k):
@@ -36,7 +55,7 @@
     count = out.shape[0]
     window[...] = jnp.zeros_like(window)
     for k, source in enumerate((low, own, high)):
-        window[k * planes : (k + 1) * planes, :] = source[0]
+        window[k * planes : (k + 1) * planes, :] = source[CHUNK]
     cells = window.shape[1]
     span = 3 * LANES * NZ // math.gcd(3 * LANES, NZ)
     assert cells % span == 0
@@ -80,21 +99,6 @@
         return carry
 
     lax.fori_loop(0, cells // span, body, 0)
-
-
-def stencil_terms(low, own, high, centre, radius):
-    planes, cells = own.shape[1:]
-    inner = 3 * planes - 2
-    smem, vmem = pl.BlockSpec(memory_space=pltpu.SMEM), pl.BlockSpec(memory_space=pltpu.VMEM)
-    return pl.pallas_call(
-        functools.partial(terms_kernel, planes),
-        out_shape=jax.ShapeDtypeStruct((inner, 8, cells), jnp.float32),
-        in_specs=[smem] + [vmem] * 3,
-        out_specs=vmem,
-        scratch_shapes=[pltpu.VMEM((24, cells), jnp.float32)],
-        compiler_params=pltpu.CompilerParams(vmem_limit_bytes=24 * 2**20),
-        name="stencil_terms",
-    )(jnp.stack([2.0 / radius, centre]), low, own, high)
 
 
 def filter_kernel(planes, halves, low, own, high, terms, out, y0, y1, y2, y3):
@@ -166,26 +170,108 @@
     sweep(y3, lambda w: w - 3, y2, lambda w: w - 2, out, 4, False)
 
 
-def filtered(low, own, high, terms, blocks):
+def first_filter_kernel(planes, halves, scales, low, own, high, out, terms, *scratch):
+    *fields, window = scratch
+    terms_kernel(planes, scales, low, own, high, terms, window)
+    filter_kernel(planes, halves, low, own, high, terms, out, *fields)
+
+
+def filtered(low, own, high, blocks, terms=None, scales=None):
     planes, cells = own.shape[1:]
     halves = blocks // planes
     width = cells // halves
     steps = (3 * planes, 3 * planes - 2, 3 * planes - 4, 3 * planes - 6)
     vmem = pl.BlockSpec(memory_space=pltpu.VMEM)
-    return pl.pallas_call(
-        functools.partial(filter_kernel, planes, halves),
-        out_shape=jax.ShapeDtypeStruct((blocks, CHUNK, width), jnp.float32),
-        in_specs=[vmem] * 4,
-        out_specs=vmem,
-        scratch_shapes=[pltpu.VMEM((count, CHUNK, cells), jnp.float32) for count in steps],
+    part = jax.ShapeDtypeStruct((blocks, CHUNK, width), jnp.float32)
+    scratch = [pltpu.VMEM((count, CHUNK, cells), jnp.float32) for count in steps]
+    options = dict(
         compiler_params=pltpu.CompilerParams(vmem_limit_bytes=32 * 2**20),
         cost_estimate=pl.CostEstimate(
             flops=14 * 7 * planes * CHUNK * cells,
             bytes_accessed=4 * 44 * CHUNK * cells,
             transcendentals=0,
         ),
-        name="chebyshev",
-    )(low, own, high, terms)
+    )
+    if scales is None:
+        return pl.pallas_call(
+            functools.partial(filter_kernel, planes, halves),
+            out_shape=part,
+            in_specs=[vmem] * 4,
+            out_specs=vmem,
+            scratch_shapes=scratch,
+            name="chebyshev",
+            **options,
+        )(low, own, high, terms)
+    return pl.pallas_call(
+        functools.partial(first_filter_kernel, planes, halves),
+        out_shape=[part, jax.ShapeDtypeStruct((3 * planes - 2, 8, cells), jnp.float32)],
+        in_specs=[pl.BlockSpec(memory_space=pltpu.SMEM)] + [vmem] * 3,
+        out_specs=[vmem] * 2,
+        scratch_shapes=scratch + [pltpu.VMEM((24, cells), jnp.float32)],
+        name="first_chebyshev",
+        **options,
+    )(scales, low, own, high)
+
+
+def rows_in_order(chunks):
+    blocks = chunks[0].shape[0]
+    return jnp.concatenate([c[b] for b in range(blocks) for c in chunks], axis=0)
+
+
+def gram_kernel(*refs):
+    *chunks, out = refs
+    field = rows_in_order(chunks)
+    update = lax.dot_general(
+        field, field, (((1,), (1,)), ((), ())), precision=HIGHEST,
+        preferred_element_type=jnp.float32,
+    ).reshape(out.shape)
+
+    @pl.when(pl.program_id(0) == 0)
+    def _():
+        out[...] = update
+
+    @pl.when(pl.program_id(0) > 0)
+    def _():
+        out[...] += update
+
+
+def partial_gram(chunks, pieces):
+    blocks, rows, width = chunks[0].shape
+    rank = blocks * rows * len(chunks)
+    shape = (pieces, rank // pieces, rank)
+    return pl.pallas_call(
+        gram_kernel,
+        grid=(width // BLOCK,),
+        out_shape=jax.ShapeDtypeStruct(shape, jnp.float32),
+        in_specs=[pl.BlockSpec((blocks, rows, BLOCK), lambda i: (0, 0, i))] * len(chunks),
+        out_specs=pl.BlockSpec(shape, lambda i: (0, 0, 0)),
+        compiler_params=pltpu.CompilerParams(vmem_limit_bytes=32 * 2**20),
+        name="partial_gram",
+    )(*chunks)
+
+
+def product_kernel(inverse, *refs):
+    *chunks, out = refs
+    result = jnp.dot(
+        inverse[...], rows_in_order(chunks), precision=HIGHEST,
+        preferred_element_type=jnp.float32,
+    )
+    out[...] = result.reshape(out.shape)
+
+
+def product(inverse, chunks):
+    blocks, rows, width = chunks[0].shape
+    rank = inverse.shape[0]
+    return pl.pallas_call(
+        product_kernel,
+        grid=(width // BLOCK,),
+        out_shape=jax.ShapeDtypeStruct((blocks, rank // blocks, width), jnp.float32),
+        in_specs=[pl.BlockSpec((rank, rank), lambda i: (0, 0))]
+        + [pl.BlockSpec((blocks, rows, BLOCK), lambda i: (0, 0, i))] * len(chunks),
+        out_specs=pl.BlockSpec((blocks, rank // blocks, BLOCK), lambda i: (0, 0, i)),
+        compiler_params=pltpu.CompilerParams(vmem_limit_bytes=32 * 2**20),
+        name="product",
+    )(inverse, *chunks)
 
 
 def assemble_kernel(planes, source, out):
@@ -210,30 +296,59 @@
 def inverse_factor_kernel(scale, gram, out, work):
     rank = gram.shape[0]
     work[...] = gram[...] * scale
-    lane = lax.broadcasted_iota(jnp.int32, (8, rank), 1)
-    sub = lax.broadcasted_iota(jnp.int32, (8, 1), 0)
+    lane = lax.broadcasted_iota(jnp.int32, (8, LANES), 1)
+    sub = lax.broadcasted_iota(jnp.int32, (8, LANES), 0)
+    wide = (8, LANES)
+    parts = rank // LANES
+    count = PANEL // 8
     for k0 in range(0, rank, PANEL):
-        groups = [work[k0 + 8 * g : k0 + 8 * g + 8, :] for g in range(PANEL // 8)]
-        pivots = [jnp.ones((8, 1), jnp.float32)] * len(groups)
-        for j in range(PANEL):
-            at, inner, column = j // 8, j % 8, k0 + j
-            here = lane == column
-            pivot = groups[at][inner : inner + 1, column : column + 1]
-            inverse = 1.0 / pivot
-            pivots[at] = jnp.where(sub == inner, pivot, pivots[at])
-            row = jnp.where(here[:1], 1.0, groups[at][inner : inner + 1, :]) * inverse
-            for g in range(at, len(groups)):
-                factor = groups[g][:, column : column + 1]
-                if g == at:
-                    factor = jnp.where(sub > inner, factor, 0.0)
-                    kept = jnp.where(here, jnp.where(sub == inner, 1.0, 0.0), groups[g])
-                    if inner:
-                        kept = jnp.where(sub < inner, groups[g], kept)
-                else:
-                    kept = jnp.where(here, 0.0, groups[g])
-                groups[g] = kept - factor * row
-        scaled = [v / jnp.sqrt(p) for v, p in zip(groups, pivots)]
-        panel = jnp.concatenate(scaled, axis=0)
+        groups = [
+            [work[k0 + 8 * g : k0 + 8 * g + 8, LANES * h : LANES * h + LANES] for h in range(parts)]
+            for g in range(count)
+        ]
+        pivots = []
+        for at in range(count):
+            first = k0 + 8 * at
+            home, start = first // LANES, first % LANES
+            spread = {
+                g: [
+                    jnp.broadcast_to(groups[g][home][:, start + j : start + j + 1], wide)
+                    for j in range(8)
+                ]
+                for g in range(at, count)
+            }
+            kept_pivots = jnp.ones(wide, jnp.float32)
+            for j in range(8):
+                pivot = jnp.broadcast_to(spread[at][j][j : j + 1, :], wide)
+                inverse = 1.0 / pivot
+                kept_pivots = jnp.where(sub == j, pivot, kept_pivots)
+                here = lane == start + j
+                rows = [jnp.broadcast_to(v[j : j + 1, :], wide) for v in groups[at]]
+                rows[home] = jnp.where(here, 1.0, rows[home])
+                later = {
+                    i: jnp.broadcast_to(spread[at][i][j : j + 1, :], wide) for i in range(j + 1, 8)
+                }
+                for g in range(at, count):
+                    factor = spread[g][j] * inverse
+                    kept = list(groups[g])
+                    if g == at:
+                        factor = jnp.where(sub > j, factor, 0.0)
+                        kept[home] = jnp.where(
+                            here & (sub >= j), jnp.where(sub == j, 1.0, 0.0), kept[home]
+                        )
+                    else:
+                        kept[home] = jnp.where(here, 0.0, kept[home])
+                    groups[g] = [v - factor * r for v, r in zip(kept, rows)]
+                    for i in range(j + 1, 8):
+                        spread[g][i] = spread[g][i] - factor * later[i]
+            pivots.append(1.0 / jnp.sqrt(kept_pivots))
+        panel = jnp.concatenate(
+            [
+                jnp.concatenate([v * p for v in group], axis=1)
+                for group, p in zip(groups, pivots)
+            ],
+            axis=0,
+        )
         done = k0 + PANEL
         columns = lax.broadcasted_iota(jnp.int32, (PANEL, rank), 1)
         rows = k0 + lax.broadcasted_iota(jnp.int32, (PANEL, rank), 0)
@@ -276,32 +391,29 @@
     up, back = neighbours("space")
     chunks = per_device // CHUNK
 
-    conduct = lookup(phase_labels, phase_conductivity)
+    scales = jnp.stack([2.0 / radius, centre])
     received = []
     for c in range(chunks):
-        own = start_vectors[c * CHUNK : (c + 1) * CHUNK]
         if c == 0:
-            own = jnp.concatenate([own, conduct[None]], axis=0)
+            own = first_chunk(start_vectors, phase_labels, phase_conductivity)
+        else:
+            own = start_vectors[c * CHUNK : (c + 1) * CHUNK]
         low = lax.ppermute(own, "space", up)
         high = lax.ppermute(own, "space", back)
         if c == 0:
-            terms = stencil_terms(
-                low[CHUNK:], conduct[None], high[CHUNK:], centre, radius
-            )
-        part = filtered(low, own, high, terms, blocks)
+            part, terms = filtered(low, own, high, blocks, scales=scales)
+        else:
+            part = filtered(low, own, high, blocks, terms=terms)
         received.append(lax.all_to_all(part, "block", 0, 0, tiled=True))
-    field = jnp.stack(received, axis=1).reshape(rank, width)
-
-    partial = jnp.einsum("mp,np->mn", field, field, precision=HIGHEST)
     devices = blocks * slabs
-    pieces = partial.reshape(devices, rank // devices, rank)
+    pieces = partial_gram(received, devices)
     summed = jnp.sum(lax.all_to_all(pieces, ("space", "block"), 0, 0, tiled=True), axis=0)
     gram = lax.all_to_all(
         jnp.broadcast_to(summed[None], pieces.shape), ("space", "block"), 0, 0, tiled=True
     ).reshape(rank, rank)
     inverse = inverse_factor(gram, 1.0 / cells)
-    result = jnp.einsum("mn,np->mp", inverse, field, precision=HIGHEST)
-    sent = lax.all_to_all(result.reshape(blocks, per_device, width), "block", 0, 0, tiled=True)
+    result = product(inverse, received)
+    sent = lax.all_to_all(result, "block", 0, 0, tiled=True)
     return assembled(sent.reshape(planes, halves, per_device, width))
 
 

time: 292 us -> 274 us (0.938)
  matrix products: 9.99 us -> 0 us
  waiting for transfers between devices: 31.2 us -> 21.5 us
  blocking collectives: 103 us -> 108 us
  other arithmetic: 5.31 us -> 0.78 us
    pallas_call x1 -> x4, Pallas kernels: 5.02 us -> 31.1 us  [the longest x1 16.1 us: filtered(): pl.pallas_call(functools.partial(first_filter_kernel, planes, halves), ou...]
    ppermute x4, waiting for transfers between devices: 18.9 us -> 1.71 us  [local(): low = lax.ppermute(own, 'space', up)]
    pallas_call x1, Pallas kernels: 26.5 us -> 10.2 us  [inverse_factor(): pl.pallas_call(functools.partial(inverse_factor_kernel, scale), out_shape...]
    pallas_call x4 -> x3, Pallas kernels: 50.9 us -> 38.5 us  [filtered(): pl.pallas_call(functools.partial(filter_kernel, planes, halves), out_shap...]
    dot_general x2 -> x0, matrix products: 9.99 us -> none  [the longest x1 6.02 us: local(): result = jnp.einsum('mn,np->mp', inverse, field, precision=HIGHEST)]
    ppermute x4, waiting for transfers between devices: 12.3 us -> 19.8 us  [local(): high = lax.ppermute(own, 'space', back)]
    unnamed x26, local copies, waits for them, and re-layouts: 8.85 us -> 13.8 us
    all_to_all x1, blocking collectives: 12.3 us -> 17 us  [local(): lax.all_to_all(pieces, ('space', 'block'), 0, 0, tiled=True)]
  transfers between devices with their start and end apart: 11 -> 11, of which waited for: 5 -> 4; matrix products, arithmetic and copies ran while one was open for 1% -> 2% of each run, Pallas kernels for 19% -> 20%
where the time goes in v1:
time: 274 us; the launch traced here: 273 us
  blocking collectives  108 us (39%)
  Pallas kernels  82.7 us (30%)
  starting transfers between devices  40.9 us (15%)
  waiting for transfers between devices  21.5 us (8%)
  local copies, waits for them, and re-layouts  17.7 us (6%)
    all_to_all x1, blocking collectives, local(): sent = lax.all_to_all(result, 'block', 0, 0, tiled=True)  57.2 us
    pallas_call x3, Pallas kernels, filtered(): pl.pallas_call(functools.partial(filter_kernel, planes, halves), out_shap...  38.5 us
    ppermute x4, starting transfers between devices, local(): low = lax.ppermute(own, 'space', up)  22.9 us
    all_to_all x1, blocking collectives, local(): received.append(lax.all_to_all(part, 'block', 0, 0, tiled=True))  20.6 us
    ppermute x4, waiting for transfers between devices, local(): high = lax.ppermute(own, 'space', back)  19.8 us
    all_to_all x1, blocking collectives, local(): lax.all_to_all(pieces, ('space', 'block'), 0, 0, tiled=True)  17 us
    pallas_call x1, Pallas kernels, filtered(): pl.pallas_call(functools.partial(first_filter_kernel, planes, halves), ou...  16.1 us
    unnamed x26, local copies, waits for them, and re-layouts  13.8 us
  transfers between devices with their start and end apart: 11, of which 4 were waited for; matrix products, arithmetic and copies ran while one was open for 2% of the time, Pallas kernels for 20%

profile of v1, /device:TPU:0, one launch (start us, length us, event | category | flops | bytes accessed | tf_op | source)
XLA Modules:
  0.0 272.9 jit_solution(11919663687596329561)
XLA Ops:
  0.0 2.5 first_chunk.1.own
  2.5 1.4 collective-permute-start.1
  3.9 5.6 %collective-permute-start = (f32[9,4,9216]{2,1,0:T(4,128)}, f32[9,4,9216]{2,1,0:T(4,128)S(1)}, u32[]{:S(2)}, u32[]{:S(2)}) collective-permute-start(f32[9,4,9216]{2,1,0:T(4,128)} %first_chunk.1.own), channel_id=1, source_target_pairs={{0,8},{8,16},{16,24},{1,9},{9,17},{17,25},{2,10},{10,18},{18,26},{... | collective-permute-start | bytes 3981320 | tf_op jit(solution)/shard_map/ppermute | solution.py:401
  9.6 3.9 %fusion = (f32[8,4,9216]{2,1,0:T(4,128)}, f32[8,4,9216]{2,1,0:T(4,128)}, f32[8,4,9216]{2,1,0:T(4,128)}) fusion(f32[32,4,9216]{2,1,0:T(4,128)} %vectors.1), kind=kLoop, calls=%fused_computation.1 | loop fusion | bytes 7077888 | tf_op jit(solution)/shard_map/slice | solution.py:400
  14.8 5.6 %collective-permute-start.6 = (f32[8,4,9216]{2,1,0:T(4,128)}, f32[8,4,9216]{2,1,0:T(4,128)}, u32[]{:S(2)}, u32[]{:S(2)}) collective-permute-start(f32[8,4,9216]{2,1,0:T(4,128)} %get-tuple-element.9.own), channel_id=1, source_target_pairs={{0,8},{8,16},{16,24},{1,9},{9,17},{17,25},{2,10},{10,18},{18,26},{... | collective-permute-start | bytes 3538952 | tf_op jit(solution)/shard_map/ppermute | solution.py:401
  22.5 15.2 %collective-permute-done.1.high = f32[9,4,9216]{2,1,0:T(4,128)S(1)} collective-permute-done((f32[9,4,9216]{2,1,0:T(4,128)}, f32[9,4,9216]{2,1,0:T(4,128)S(1)}, u32[]{:S(2)}, u32[]{:S(2)}) %collective-permute-start.1) | collective-permute-done | bytes 1327136 | tf_op jit(solution)/shard_map/ppermute | solution.py:402
  44.5 16.1 %first_chebyshev.1 = (f32[8,8,4608]{2,1,0:T(8,128)S(1)}, f32[10,8,9216]{2,1,0:T(8,128)S(1)}) custom-call(f32[2]{0:T(128)S(1)} %pad_maximum_fusion.scales, f32[9,4,9216]{2,1,0:T(4,128)S(1)} %copy-done.9, f32[9,4,9216]{2,1,0:T(4,128)S(1)} %copy-done, f32[9,4,9216]{2,1,0:T(4,128)S(1)} %copy-done.7), custom_call_target="tpu_custom_call" | custom-call | flops 28901376 | bytes 12976128 | tf_op jit(solution)/shard_map/first_chebyshev/pallas_call | solution.py:205
  61.6 4.3 %all-to-all-start = ((f32[8,8,4608]{2,1,0:T(8,128)}), f32[8,8,4608]{2,1,0:T(8,128)}, u32[]{:S(2)}, u32[]{:S(2)}) async-start(f32[8,8,4608]{2,1,0:T(8,128)} %copy-done.10), calls=%async_computation | async-start | bytes 2359296 | tf_op jit(solution)/shard_map/all_to_all | solution.py:407
  67.1 6.0 %collective-permute-start.2 = (f32[8,4,9216]{2,1,0:T(4,128)}, f32[8,4,9216]{2,1,0:T(4,128)}, u32[]{:S(2)}, u32[]{:S(2)}) collective-permute-start(f32[8,4,9216]{2,1,0:T(4,128)} %get-tuple-element.10.own), channel_id=1, source_target_pairs={{0,8},{8,16},{16,24},{1,9},{9,17},{17,25},{2,10},{10,18},{18,26},{... | collective-permute-start | bytes 3538952 | tf_op jit(solution)/shard_map/ppermute | solution.py:401
  73.1 13.1 %chebyshev.5 = f32[8,8,4608]{2,1,0:T(8,128)S(1)} custom-call(f32[8,4,9216]{2,1,0:T(4,128)} %collective-permute-done.6.low, f32[8,4,9216]{2,1,0:T(4,128)} %get-tuple-element.9.own, f32[8,4,9216]{2,1,0:T(4,128)} %collective-permute-done.7.high, f32[10,8,9216]{2,1,0:T(8,128)S(1)} %get-tuple-element.8.terms), custom_call_target="tpu_custom_call" | custom-call | flops 28901376 | bytes 12976128 | tf_op jit(solution)/shard_map/chebyshev/pallas_call | solution.py:196
  87.2 4.2 %all-to-all-start.3 = ((f32[8,8,4608]{2,1,0:T(8,128)}), f32[8,8,4608]{2,1,0:T(8,128)}, u32[]{:S(2)}, u32[]{:S(2)}) async-start(f32[8,8,4608]{2,1,0:T(8,128)} %copy-done.3), calls=%async_computation.3 | async-start | bytes 2359296 | tf_op jit(solution)/shard_map/all_to_all | solution.py:407
  92.8 5.6 %collective-permute-start.4 = (f32[8,4,9216]{2,1,0:T(4,128)}, f32[8,4,9216]{2,1,0:T(4,128)}, u32[]{:S(2)}, u32[]{:S(2)}) collective-permute-start(f32[8,4,9216]{2,1,0:T(4,128)} %get-tuple-element.11.own), channel_id=1, source_target_pairs={{0,8},{8,16},{16,24},{1,9},{9,17},{17,25},{2,10},{10,18},{18,26},{... | collective-permute-start | bytes 3538952 | tf_op jit(solution)/shard_map/ppermute | solution.py:401
  99.7 12.7 %chebyshev.3 = f32[8,8,4608]{2,1,0:T(8,128)S(1)} custom-call(f32[8,4,9216]{2,1,0:T(4,128)} %collective-permute-done.2.low, f32[8,4,9216]{2,1,0:T(4,128)S(1)} %copy-done.2, f32[8,4,9216]{2,1,0:T(4,128)} %collective-permute-done.3.high, f32[10,8,9216]{2,1,0:T(8,128)S(1)} %get-tuple-element.8.terms), custom_call_target="tpu_custom_call" | custom-call | flops 28901376 | bytes 12976128 | tf_op jit(solution)/shard_map/chebyshev/pallas_call | solution.py:196
  113.4 4.2 %all-to-all-start.1 = ((f32[8,8,4608]{2,1,0:T(8,128)}), f32[8,8,4608]{2,1,0:T(8,128)}, u32[]{:S(2)}, u32[]{:S(2)}) async-start(f32[8,8,4608]{2,1,0:T(8,128)} %copy-done.4), calls=%async_computation.1 | async-start | bytes 2359296 | tf_op jit(solution)/shard_map/all_to_all | solution.py:407
  117.7 4.6 %collective-permute-done.5.high = f32[8,4,9216]{2,1,0:T(4,128)} collective-permute-done((f32[8,4,9216]{2,1,0:T(4,128)}, f32[8,4,9216]{2,1,0:T(4,128)}, u32[]{:S(2)}, u32[]{:S(2)}) %collective-permute-start.5) | collective-permute-done | bytes 1179680 | tf_op jit(solution)/shard_map/ppermute | solution.py:402
  124.7 12.7 %chebyshev.4 = f32[8,8,4608]{2,1,0:T(8,128)S(1)} custom-call(f32[8,4,9216]{2,1,0:T(4,128)} %collective-permute-done.4.low, f32[8,4,9216]{2,1,0:T(4,128)S(1)} %copy-done.1, f32[8,4,9216]{2,1,0:T(4,128)} %collective-permute-done.5.high, f32[10,8,9216]{2,1,0:T(8,128)S(1)} %get-tuple-element.8.terms), custom_call_target="tpu_custom_call" | custom-call | flops 28901376 | bytes 12976128 | tf_op jit(solution)/shard_map/chebyshev/pallas_call | solution.py:196
  138.5 20.6 %all_to_all.35.refs_2_ = f32[8,8,4608]{2,1,0:T(8,128)S(1)} all-to-all(f32[8,8,4608]{2,1,0:T(8,128)} %copy-done.5), channel_id=1, replica_groups=mesh['space'=4,'block'=8] {'block'}, dimensions={0} | all-to-all | bytes 2359296 | tf_op jit(solution)/shard_map/all_to_all | solution.py:407
  159.1 6.2 %partial_gram.1 = f32[32,8,256]{2,1,0:T(8,128)S(1)} custom-call(f32[8,8,4608]{2,1,0:T(8,128)} %all-to-all-done.refs_0_, f32[8,8,4608]{2,1,0:T(8,128)} %all-to-all-done.1.refs_1_, f32[8,8,4608]{2,1,0:T(8,128)S(1)} %all_to_all.35.refs_2_, f32[8,8,4608]{2,1,0:T(8,128)} %all-to-all-done.3.refs_3_), custom_call_target="tpu_custom_call" | custom-call | tf_op jit(solution)/shard_map/partial_gram/pallas_call | solution.py:242
  165.3 17.0 %all_to_all.36 = f32[32,8,256]{2,1,0:T(8,128)S(1)} all-to-all(f32[32,8,256]{2,1,0:T(8,128)S(1)} %partial_gram.1), channel_id=1, replica_groups=mesh['space'=4,'block'=8] {'space','block'}, dimensions={0} | all-to-all | bytes 524288 | tf_op jit(solution)/shard_map/all_to_all | solution.py:410
  182.3 13.0 %all_to_all.37 = f32[32,8,256]{2,1,0:T(8,128)} all-to-all(f32[32,8,256]{2,1,0:T(8,128)S(1)} %broadcast_in_dim.2), channel_id=1, replica_groups=mesh['space'=4,'block'=8] {'space','block'}, dimensions={0} | all-to-all | bytes 524288 | tf_op jit(solution)/shard_map/all_to_all | solution.py:411
  195.3 10.2 %inverse_factor.1.inverse = f32[256,256]{1,0:T(8,128)} custom-call(f32[256,256]{1,0:T(8,128)} %bitcast.5), custom_call_target="tpu_custom_call" | custom-call | tf_op jit(solution)/shard_map/inverse_factor/pallas_call | solution.py:369
  206.5 6.3 %product.1 = f32[8,32,4608]{2,1,0:T(8,128)S(1)} custom-call(f32[256,256]{1,0:T(8,128)S(1)} %copy-done.11, f32[8,8,4608]{2,1,0:T(8,128)} %all-to-all-done.refs_0_, f32[8,8,4608]{2,1,0:T(8,128)} %all-to-all-done.1.refs_1_, f32[8,8,4608]{2,1,0:T(8,128)S(1)} %all_to_all.35.refs_2_, f32[8,8,4608]{2,1,0:T(8,128)} %all-to-all-done.3.refs_3_), custom_call_target="tpu_custom_call" | custom-call | tf_op jit(solution)/shard_map/product/pallas_call | solution.py:265
  212.8 57.2 %all_to_all.38 = f32[8,32,4608]{2,1,0:T(8,128)S(1)} all-to-all(f32[8,32,4608]{2,1,0:T(8,128)S(1)} %product.1), channel_id=1, replica_groups=mesh['space'=4,'block'=8] {'block'}, dimensions={0} | all-to-all | bytes 9437184 | tf_op jit(solution)/shard_map/all_to_all | solution.py:416
  269.9 3.0 %assemble.1 = f32[32,4,9216]{2,1,0:T(4,128)} custom-call(f32[4,2,32,4608]{3,2,1,0:T(8,128)S(1)} %bitcast.4), custom_call_target="tpu_custom_call" | custom-call | tf_op jit(solution)/shard_map/assemble/pallas_call | solution.py:285
  (42 shorter events, 20.2 us)
Async XLA Ops:
  2.5 17.9 %copy-start.12 = (f32[3]{0:T(128)S(1)}, f32[3]{0:T(128)}, u32[]{:S(2)}) copy-start(f32[3]{0:T(128)} %table.1) | copy-start | bytes 40
  2.5 35.2 %collective-permute-start.1 = (f32[9,4,9216]{2,1,0:T(4,128)}, f32[9,4,9216]{2,1,0:T(4,128)S(1)}, u32[]{:S(2)}, u32[]{:S(2)}) collective-permute-start(f32[9,4,9216]{2,1,0:T(4,128)} %first_chunk.1.own), channel_id=1, source_target_pairs={{8,0},{16,8},{24,16},{9,1},{17,9},{25,17},{10,2},{18,10},{26,18},{... | collective-permute-start | bytes 3981320 | tf_op jit(solution)/shard_map/ppermute | solution.py:402
  3.9 35.4 %collective-permute-start = (f32[9,4,9216]{2,1,0:T(4,128)}, f32[9,4,9216]{2,1,0:T(4,128)S(1)}, u32[]{:S(2)}, u32[]{:S(2)}) collective-permute-start(f32[9,4,9216]{2,1,0:T(4,128)} %first_chunk.1.own), channel_id=1, source_target_pairs={{0,8},{8,16},{16,24},{1,9},{9,17},{17,25},{2,10},{10,18},{18,26},{... | collective-permute-start | bytes 3981320 | tf_op jit(solution)/shard_map/ppermute | solution.py:401
  13.5 59.6 %collective-permute-start.7 = (f32[8,4,9216]{2,1,0:T(4,128)}, f32[8,4,9216]{2,1,0:T(4,128)}, u32[]{:S(2)}, u32[]{:S(2)}) collective-permute-start(f32[8,4,9216]{2,1,0:T(4,128)} %get-tuple-element.9.own), channel_id=1, source_target_pairs={{8,0},{16,8},{24,16},{9,1},{17,9},{25,17},{10,2},{18,10},{26,18},{... | collective-permute-start | bytes 3538952 | tf_op jit(solution)/shard_map/ppermute | solution.py:402
  14.8 58.3 %collective-permute-start.6 = (f32[8,4,9216]{2,1,0:T(4,128)}, f32[8,4,9216]{2,1,0:T(4,128)}, u32[]{:S(2)}, u32[]{:S(2)}) collective-permute-start(f32[8,4,9216]{2,1,0:T(4,128)} %get-tuple-element.9.own), channel_id=1, source_target_pairs={{0,8},{8,16},{16,24},{1,9},{9,17},{17,25},{2,10},{10,18},{18,26},{... | collective-permute-start | bytes 3538952 | tf_op jit(solution)/shard_map/ppermute | solution.py:401
  37.7 1.1 copy-start.6
  39.3 1.1 copy-start.8
  40.5 1.3 copy-start
  41.8 1.3 copy-start.7
  43.1 1.3 copy-start.9
  60.5 1.0 copy-start.10
  61.6 25.7 %all-to-all-start = ((f32[8,8,4608]{2,1,0:T(8,128)}), f32[8,8,4608]{2,1,0:T(8,128)}, u32[]{:S(2)}, u32[]{:S(2)}) async-start(f32[8,8,4608]{2,1,0:T(8,128)} %copy-done.10), calls=%async_computation | async-start | bytes 2359296 | tf_op jit(solution)/shard_map/all_to_all | solution.py:407
  65.8 32.6 %collective-permute-start.3 = (f32[8,4,9216]{2,1,0:T(4,128)}, f32[8,4,9216]{2,1,0:T(4,128)}, u32[]{:S(2)}, u32[]{:S(2)}) collective-permute-start(f32[8,4,9216]{2,1,0:T(4,128)} %get-tuple-element.10.own), channel_id=1, source_target_pairs={{8,0},{16,8},{24,16},{9,1},{17,9},{25,17},{10,2},{18,10},{26,18},{... | collective-permute-start | bytes 3538952 | tf_op jit(solution)/shard_map/ppermute | solution.py:402
  67.1 31.3 %collective-permute-start.2 = (f32[8,4,9216]{2,1,0:T(4,128)}, f32[8,4,9216]{2,1,0:T(4,128)}, u32[]{:S(2)}, u32[]{:S(2)}) collective-permute-start(f32[8,4,9216]{2,1,0:T(4,128)} %get-tuple-element.10.own), channel_id=1, source_target_pairs={{0,8},{8,16},{16,24},{1,9},{9,17},{17,25},{2,10},{10,18},{18,26},{... | collective-permute-start | bytes 3538952 | tf_op jit(solution)/shard_map/ppermute | solution.py:401
  86.2 1.1 copy-start.3
  87.2 26.2 %all-to-all-start.3 = ((f32[8,8,4608]{2,1,0:T(8,128)}), f32[8,8,4608]{2,1,0:T(8,128)}, u32[]{:S(2)}, u32[]{:S(2)}) async-start(f32[8,8,4608]{2,1,0:T(8,128)} %copy-done.3), calls=%async_computation.3 | async-start | bytes 2359296 | tf_op jit(solution)/shard_map/all_to_all | solution.py:407
  91.5 30.8 %collective-permute-start.5 = (f32[8,4,9216]{2,1,0:T(4,128)}, f32[8,4,9216]{2,1,0:T(4,128)}, u32[]{:S(2)}, u32[]{:S(2)}) collective-permute-start(f32[8,4,9216]{2,1,0:T(4,128)} %get-tuple-element.11.own), channel_id=1, source_target_pairs={{8,0},{16,8},{24,16},{9,1},{17,9},{25,17},{10,2},{18,10},{26,18},{... | collective-permute-start | bytes 3538952 | tf_op jit(solution)/shard_map/ppermute | solution.py:402
  92.8 30.7 %collective-permute-start.4 = (f32[8,4,9216]{2,1,0:T(4,128)}, f32[8,4,9216]{2,1,0:T(4,128)}, u32[]{:S(2)}, u32[]{:S(2)}) collective-permute-start(f32[8,4,9216]{2,1,0:T(4,128)} %get-tuple-element.11.own), channel_id=1, source_target_pairs={{0,8},{8,16},{16,24},{1,9},{9,17},{17,25},{2,10},{10,18},{18,26},{... | collective-permute-start | bytes 3538952 | tf_op jit(solution)/shard_map/ppermute | solution.py:401
  98.4 1.3 copy-start.2
  112.4 1.0 copy-start.4
  113.4 25.0 %all-to-all-start.1 = ((f32[8,8,4608]{2,1,0:T(8,128)}), f32[8,8,4608]{2,1,0:T(8,128)}, u32[]{:S(2)}, u32[]{:S(2)}) async-start(f32[8,8,4608]{2,1,0:T(8,128)} %copy-done.4), calls=%async_computation.1 | async-start | bytes 2359296 | tf_op jit(solution)/shard_map/all_to_all | solution.py:407
  123.5 1.3 copy-start.1
  137.4 1.0 copy-start.5
  205.5 0.9 copy-start.11

commit v2 on v1

--- a/solution.py
+++ b/solution.py
@@ -50,12 +50,12 @@
     return 2.0 * left_k * filled / (left_k + filled)
 
 
-def terms_kernel(planes, scales, low, own, high, out, window):
+def terms_kernel(planes, scales, raw, out, window):
     scale, shift = scales[0], scales[1]
     count = out.shape[0]
     window[...] = jnp.zeros_like(window)
-    for k, source in enumerate((low, own, high)):
-        window[k * planes : (k + 1) * planes, :] = source[CHUNK]
+    for k in range(3):
+        window[k * planes : (k + 1) * planes, :] = raw[k, CHUNK]
     cells = window.shape[1]
     span = 3 * LANES * NZ // math.gcd(3 * LANES, NZ)
     assert cells % span == 0
@@ -101,10 +101,19 @@
     lax.fori_loop(0, cells // span, body, 0)
 
 
-def filter_kernel(planes, halves, low, own, high, terms, out, y0, y1, y2, y3):
-    for k, source in enumerate((low, own, high)):
+def start_reading(sources, raw, sems):
+    copies = [
+        pltpu.make_async_copy(source, raw.at[k], sems.at[k]) for k, source in enumerate(sources)
+    ]
+    for copy in copies:
+        copy.start()
+    return copies
+
+
+def filter_kernel(planes, halves, raw, terms, target_array, out, sems, y0, y1, y2, y3):
+    for k in range(3):
         for p in range(planes):
-            y0[k * planes + p] = source[0:CHUNK, p, :]
+            y0[k * planes + p] = raw[k, 0:CHUNK, p, :]
     cells = y0.shape[-1]
     tiles = cells // LANES
     per_half = tiles // halves
@@ -157,35 +166,73 @@
                     target[p, :, span] = result
                 return carry
 
-            return lax.fori_loop(0, tiles // group, group_body, carry, unroll=True)
+            lax.fori_loop(0, tiles // group, group_body, 0, unroll=True)
+            if target is out:
+                leaving(p).start()
+            return carry
 
         lax.fori_loop(0, count, plane_body, 0)
 
     def target_planes(target):
         return planes if target is out else target.shape[0]
+
+    def leaving(p):
+        rows = pl.ds(p * halves, halves)
+        return pltpu.make_async_copy(out.at[rows], target_array.at[rows], sems.at[p])
 
     sweep(y0, lambda w: w, None, None, y1, 1, True)
     sweep(y1, lambda w: w - 1, y0, lambda w: w, y2, 2, False)
     sweep(y2, lambda w: w - 2, y1, lambda w: w - 1, y3, 3, False)
     sweep(y3, lambda w: w - 3, y2, lambda w: w - 2, out, 4, False)
-
-
-def first_filter_kernel(planes, halves, scales, low, own, high, out, terms, *scratch):
-    *fields, window = scratch
-    terms_kernel(planes, scales, low, own, high, terms, window)
-    filter_kernel(planes, halves, low, own, high, terms, out, *fields)
+    for p in range(planes):
+        leaving(p).wait()
+
+
+def next_filter_kernel(
+    planes, halves, low, own, high, stored, target, raw, sems, out, y0, y1, y2, y3, terms
+):
+    copies = start_reading((low, own, high), raw, sems)
+    last = pltpu.make_async_copy(stored, terms, sems.at[3 + planes])
+    last.start()
+    for copy in copies:
+        copy.wait()
+    last.wait()
+    filter_kernel(
+        planes, halves, raw, terms, target, out, sems.at[pl.ds(3, planes)], y0, y1, y2, y3
+    )
+
+
+def first_filter_kernel(
+    planes, halves, scales, low, own, high, target, stored, raw, sems, out, y0, y1, y2, y3, terms, window
+):
+    for copy in start_reading((low, own, high), raw, sems):
+        copy.wait()
+    terms_kernel(planes, scales, raw, terms, window)
+    last = pltpu.make_async_copy(terms, stored, sems.at[3 + planes])
+    last.start()
+    filter_kernel(
+        planes, halves, raw, terms, target, out, sems.at[pl.ds(3, planes)], y0, y1, y2, y3
+    )
+    last.wait()
 
 
 def filtered(low, own, high, blocks, terms=None, scales=None):
-    planes, cells = own.shape[1:]
+    rows, planes, cells = own.shape
     halves = blocks // planes
     width = cells // halves
     steps = (3 * planes, 3 * planes - 2, 3 * planes - 4, 3 * planes - 6)
-    vmem = pl.BlockSpec(memory_space=pltpu.VMEM)
+    hbm = pl.BlockSpec(memory_space=pltpu.HBM)
     part = jax.ShapeDtypeStruct((blocks, CHUNK, width), jnp.float32)
-    scratch = [pltpu.VMEM((count, CHUNK, cells), jnp.float32) for count in steps]
+    scratch = [
+        pltpu.VMEM((3, rows, planes, cells), jnp.float32),
+        pltpu.SemaphoreType.DMA((4 + planes,)),
+        pltpu.VMEM(part.shape, jnp.float32),
+    ]
+    scratch += [pltpu.VMEM((count, CHUNK, cells), jnp.float32) for count in steps]
+    factors = jax.ShapeDtypeStruct((3 * planes - 2, 8, cells), jnp.float32)
+    scratch.append(pltpu.VMEM(factors.shape, jnp.float32))
     options = dict(
-        compiler_params=pltpu.CompilerParams(vmem_limit_bytes=32 * 2**20),
+        compiler_params=pltpu.CompilerParams(vmem_limit_bytes=60 * 2**20),
         cost_estimate=pl.CostEstimate(
             flops=14 * 7 * planes * CHUNK * cells,
             bytes_accessed=4 * 44 * CHUNK * cells,
@@ -194,19 +241,19 @@
     )
     if scales is None:
         return pl.pallas_call(
-            functools.partial(filter_kernel, planes, halves),
+            functools.partial(next_filter_kernel, planes, halves),
             out_shape=part,
-            in_specs=[vmem] * 4,
-            out_specs=vmem,
+            in_specs=[hbm] * 4,
+            out_specs=hbm,
             scratch_shapes=scratch,
             name="chebyshev",
             **options,
         )(low, own, high, terms)
     return pl.pallas_call(
         functools.partial(first_filter_kernel, planes, halves),
-        out_shape=[part, jax.ShapeDtypeStruct((3 * planes - 2, 8, cells), jnp.float32)],
-        in_specs=[pl.BlockSpec(memory_space=pltpu.SMEM)] + [vmem] * 3,
-        out_specs=[vmem] * 2,
+        out_shape=[part, factors],
+        in_specs=[pl.BlockSpec(memory_space=pltpu.SMEM)] + [hbm] * 3,
+        out_specs=[hbm] * 2,
         scratch_shapes=scratch + [pltpu.VMEM((24, cells), jnp.float32)],
         name="first_chebyshev",
         **options,
@@ -245,18 +292,24 @@
         out_shape=jax.ShapeDtypeStruct(shape, jnp.float32),
         in_specs=[pl.BlockSpec((blocks, rows, BLOCK), lambda i: (0, 0, i))] * len(chunks),
         out_specs=pl.BlockSpec(shape, lambda i: (0, 0, 0)),
-        compiler_params=pltpu.CompilerParams(vmem_limit_bytes=32 * 2**20),
+        compiler_params=pltpu.CompilerParams(vmem_limit_bytes=60 * 2**20),
         name="partial_gram",
     )(*chunks)
 
 
+def halved(value):
+    high = value.astype(jnp.bfloat16)
+    return high, (value - high.astype(jnp.float32)).astype(jnp.bfloat16)
+
+
+def dot(left, right):
+    return jnp.dot(left, right, preferred_element_type=jnp.float32)
+
+
 def product_kernel(inverse, *refs):
     *chunks, out = refs
-    result = jnp.dot(
-        inverse[...], rows_in_order(chunks), precision=HIGHEST,
-        preferred_element_type=jnp.float32,
-    )
-    out[...] = result.reshape(out.shape)
+    (a, b), (x, y) = halved(inverse[...]), halved(rows_in_order(chunks))
+    out[...] = (dot(a, x) + (dot(a, y) + dot(b, x))).reshape(out.shape)
 
 
 def product(inverse, chunks):
@@ -269,7 +322,7 @@
         in_specs=[pl.BlockSpec((rank, rank), lambda i: (0, 0))]
         + [pl.BlockSpec((blocks, rows, BLOCK), lambda i: (0, 0, i))] * len(chunks),
         out_specs=pl.BlockSpec((blocks, rank // blocks, BLOCK), lambda i: (0, 0, i)),
-        compiler_params=pltpu.CompilerParams(vmem_limit_bytes=32 * 2**20),
+        compiler_params=pltpu.CompilerParams(vmem_limit_bytes=60 * 2**20),
         name="product",
     )(inverse, *chunks)
 
@@ -288,7 +341,7 @@
         out_shape=jax.ShapeDtypeStruct((rows, planes, halves * width), jnp.float32),
         in_specs=[pl.BlockSpec((planes, 1, rows, width), lambda i: (0, i, 0, 0))],
         out_specs=pl.BlockSpec((rows, planes, width), lambda i: (0, 0, i)),
-        compiler_params=pltpu.CompilerParams(vmem_limit_bytes=32 * 2**20),
+        compiler_params=pltpu.CompilerParams(vmem_limit_bytes=60 * 2**20),
         name="assemble",
     )(pieces)
 

time: 274 us -> 276 us (level)
  local copies, waits for them, and re-layouts: 17.7 us -> 5.3 us
  Pallas kernels: 82.7 us -> 93.8 us
    unnamed x26 -> x12, local copies, waits for them, and re-layouts: 13.8 us -> 2.05 us
    pallas_call x3, Pallas kernels: 38.5 us -> 44.3 us  [filtered(): pl.pallas_call(functools.partial(next_filter_kernel, planes, halves), out...]
    pallas_call x1, Pallas kernels: 16.1 us -> 19.1 us  [filtered(): pl.pallas_call(functools.partial(first_filter_kernel, planes, halves), ou...]
  transfers between devices with their start and end apart: 11 -> 11, of which waited for: 4 -> 4; matrix products, arithmetic and copies ran while one was open for 2% -> 2% of each run, Pallas kernels for 20% -> 23%
where the time goes in v2:
time: 276 us; the launch traced here: 275 us
  blocking collectives  110 us (40%)
  Pallas kernels  93.8 us (34%)
  starting transfers between devices  41.8 us (15%)
  waiting for transfers between devices  20.5 us (7%)
  local copies, waits for them, and re-layouts  5.3 us (2%)
    all_to_all x1, blocking collectives, local(): sent = lax.all_to_all(result, 'block', 0, 0, tiled=True)  59.2 us
    pallas_call x3, Pallas kernels, filtered(): pl.pallas_call(functools.partial(next_filter_kernel, planes, halves), out...  44.3 us
    ppermute x4, starting transfers between devices, local(): low = lax.ppermute(own, 'space', up)  24 us
    all_to_all x1, blocking collectives, local(): received.append(lax.all_to_all(part, 'block', 0, 0, tiled=True))  21 us
    pallas_call x1, Pallas kernels, filtered(): pl.pallas_call(functools.partial(first_filter_kernel, planes, halves), ou...  19.1 us
    ppermute x4, waiting for transfers between devices, local(): high = lax.ppermute(own, 'space', back)  17.9 us
    all_to_all x1, blocking collectives, local(): lax.all_to_all(pieces, ('space', 'block'), 0, 0, tiled=True)  17.2 us
    all_to_all x1, blocking collectives, local(): lax.all_to_all(jnp.broadcast_to(summed[None], pieces.shape), ('space', 'b...  13 us
  transfers between devices with their start and end apart: 11, of which 4 were waited for; matrix products, arithmetic and copies ran while one was open for 2% of the time, Pallas kernels for 23%

profile of v2, /device:TPU:0, one launch (start us, length us, event | category | flops | bytes accessed | tf_op | source)
XLA Modules:
  0.0 274.6 jit_solution(9381471998867692772)
XLA Ops:
  0.0 2.5 first_chunk.1.own
  4.0 6.7 %collective-permute-start = (f32[9,4,9216]{2,1,0:T(4,128)}, f32[9,4,9216]{2,1,0:T(4,128)}, u32[]{:S(2)}, u32[]{:S(2)}) collective-permute-start(f32[9,4,9216]{2,1,0:T(4,128)} %first_chunk.1.own), channel_id=1, source_target_pairs={{0,8},{8,16},{16,24},{1,9},{9,17},{17,25},{2,10},{10,18},{18,26},{... | collective-permute-start | bytes 3981320 | tf_op jit(solution)/shard_map/ppermute | solution.py:454
  10.7 3.2 %fusion = (f32[8,4,9216]{2,1,0:T(4,128)S(1)}, f32[8,4,9216]{2,1,0:T(4,128)}, f32[8,4,9216]{2,1,0:T(4,128)S(1)}) fusion(f32[32,4,9216]{2,1,0:T(4,128)} %vectors.1), kind=kLoop, calls=%fused_computation.1 | loop fusion | bytes 7077888 | tf_op jit(solution)/shard_map/slice | solution.py:453
  15.2 5.6 %collective-permute-start.6 = (f32[8,4,9216]{2,1,0:T(4,128)S(1)}, f32[8,4,9216]{2,1,0:T(4,128)}, u32[]{:S(2)}, u32[]{:S(2)}) collective-permute-start(f32[8,4,9216]{2,1,0:T(4,128)S(1)} %get-tuple-element.9.own), channel_id=1, source_target_pairs={{0,8},{8,16},{16,24},{1,9},{9,17},{17,25},{2,10},{10,18},{18,26},{... | collective-permute-start | bytes 3538952 | tf_op jit(solution)/shard_map/ppermute | solution.py:454
  23.4 14.5 %collective-permute-done.1.high = f32[9,4,9216]{2,1,0:T(4,128)} collective-permute-done((f32[9,4,9216]{2,1,0:T(4,128)}, f32[9,4,9216]{2,1,0:T(4,128)}, u32[]{:S(2)}, u32[]{:S(2)}) %collective-permute-start.1) | collective-permute-done | bytes 1327136 | tf_op jit(solution)/shard_map/ppermute | solution.py:455
  37.9 1.5 collective-permute-done.low
  39.4 19.1 %first_chebyshev.1 = (f32[8,8,4608]{2,1,0:T(8,128)}, f32[10,8,9216]{2,1,0:T(8,128)}) custom-call(f32[2]{0:T(128)} %pad_maximum_fusion.scales, f32[9,4,9216]{2,1,0:T(4,128)} %collective-permute-done.low, f32[9,4,9216]{2,1,0:T(4,128)} %first_chunk.1.own, f32[9,4,9216]{2,1,0:T(4,128)} %collective-permute-done.1.high), custom_call_target="tpu_custom_call" | custom-call | flops 28901376 | bytes 12976128 | tf_op jit(solution)/shard_map/first_chebyshev/pallas_call | solution.py:252
  58.5 4.2 %all-to-all-start = ((f32[8,8,4608]{2,1,0:T(8,128)}), f32[8,8,4608]{2,1,0:T(8,128)S(1)}, u32[]{:S(2)}, u32[]{:S(2)}) async-start(f32[8,8,4608]{2,1,0:T(8,128)} %get-tuple-element.7), calls=%async_computation | async-start | bytes 2359296 | tf_op jit(solution)/shard_map/all_to_all | solution.py:460
  64.0 6.1 %collective-permute-start.2 = (f32[8,4,9216]{2,1,0:T(4,128)}, f32[8,4,9216]{2,1,0:T(4,128)}, u32[]{:S(2)}, u32[]{:S(2)}) collective-permute-start(f32[8,4,9216]{2,1,0:T(4,128)} %get-tuple-element.10.own), channel_id=1, source_target_pairs={{0,8},{8,16},{16,24},{1,9},{9,17},{17,25},{2,10},{10,18},{18,26},{... | collective-permute-start | bytes 3538952 | tf_op jit(solution)/shard_map/ppermute | solution.py:454
  70.1 14.8 %chebyshev.5 = f32[8,8,4608]{2,1,0:T(8,128)} custom-call(f32[8,4,9216]{2,1,0:T(4,128)} %collective-permute-done.6.low, f32[8,4,9216]{2,1,0:T(4,128)} %copy-done.4, f32[8,4,9216]{2,1,0:T(4,128)} %collective-permute-done.7.high, f32[10,8,9216]{2,1,0:T(8,128)} %get-tuple-element.8.stored), custom_call_target="tpu_custom_call" | custom-call | flops 28901376 | bytes 12976128 | tf_op jit(solution)/shard_map/chebyshev/pallas_call | solution.py:243
  85.9 4.2 %all-to-all-start.3 = ((f32[8,8,4608]{2,1,0:T(8,128)}), f32[8,8,4608]{2,1,0:T(8,128)S(1)}, u32[]{:S(2)}, u32[]{:S(2)}) async-start(f32[8,8,4608]{2,1,0:T(8,128)} %chebyshev.5), calls=%async_computation.3 | async-start | bytes 2359296 | tf_op jit(solution)/shard_map/all_to_all | solution.py:460
  91.4 5.6 %collective-permute-start.4 = (f32[8,4,9216]{2,1,0:T(4,128)S(1)}, f32[8,4,9216]{2,1,0:T(4,128)}, u32[]{:S(2)}, u32[]{:S(2)}) collective-permute-start(f32[8,4,9216]{2,1,0:T(4,128)S(1)} %get-tuple-element.11.own), channel_id=1, source_target_pairs={{0,8},{8,16},{16,24},{1,9},{9,17},{17,25},{2,10},{10,18},{18,26},{... | collective-permute-start | bytes 3538952 | tf_op jit(solution)/shard_map/ppermute | solution.py:454
  97.0 14.8 %chebyshev.3 = f32[8,8,4608]{2,1,0:T(8,128)} custom-call(f32[8,4,9216]{2,1,0:T(4,128)} %collective-permute-done.2.low, f32[8,4,9216]{2,1,0:T(4,128)} %get-tuple-element.10.own, f32[8,4,9216]{2,1,0:T(4,128)} %collective-permute-done.3.high, f32[10,8,9216]{2,1,0:T(8,128)} %get-tuple-element.8.stored), custom_call_target="tpu_custom_call" | custom-call | flops 28901376 | bytes 12976128 | tf_op jit(solution)/shard_map/chebyshev/pallas_call | solution.py:243
  112.8 4.2 %all-to-all-start.1 = ((f32[8,8,4608]{2,1,0:T(8,128)}), f32[8,8,4608]{2,1,0:T(8,128)S(1)}, u32[]{:S(2)}, u32[]{:S(2)}) async-start(f32[8,8,4608]{2,1,0:T(8,128)} %chebyshev.3), calls=%async_computation.1 | async-start | bytes 2359296 | tf_op jit(solution)/shard_map/all_to_all | solution.py:460
  117.0 3.4 %collective-permute-done.5.high = f32[8,4,9216]{2,1,0:T(4,128)} collective-permute-done((f32[8,4,9216]{2,1,0:T(4,128)S(1)}, f32[8,4,9216]{2,1,0:T(4,128)}, u32[]{:S(2)}, u32[]{:S(2)}) %collective-permute-start.5) | collective-permute-done | bytes 1179680 | tf_op jit(solution)/shard_map/ppermute | solution.py:455
  121.6 14.8 %chebyshev.4 = f32[8,8,4608]{2,1,0:T(8,128)} custom-call(f32[8,4,9216]{2,1,0:T(4,128)} %collective-permute-done.4.low, f32[8,4,9216]{2,1,0:T(4,128)} %copy-done.3, f32[8,4,9216]{2,1,0:T(4,128)} %collective-permute-done.5.high, f32[10,8,9216]{2,1,0:T(8,128)} %get-tuple-element.8.stored), custom_call_target="tpu_custom_call" | custom-call | flops 28901376 | bytes 12976128 | tf_op jit(solution)/shard_map/chebyshev/pallas_call | solution.py:243
  136.4 21.0 %all_to_all.35.refs_2_ = f32[8,8,4608]{2,1,0:T(8,128)} all-to-all(f32[8,8,4608]{2,1,0:T(8,128)} %chebyshev.4), channel_id=1, replica_groups=mesh['space'=4,'block'=8] {'block'}, dimensions={0} | all-to-all | bytes 2359296 | tf_op jit(solution)/shard_map/all_to_all | solution.py:460
  157.4 7.0 %partial_gram.1 = f32[32,8,256]{2,1,0:T(8,128)} custom-call(f32[8,8,4608]{2,1,0:T(8,128)} %copy-done, f32[8,8,4608]{2,1,0:T(8,128)} %copy-done.2, f32[8,8,4608]{2,1,0:T(8,128)} %all_to_all.35.refs_2_, f32[8,8,4608]{2,1,0:T(8,128)} %copy-done.1), custom_call_target="tpu_custom_call" | custom-call | tf_op jit(solution)/shard_map/partial_gram/pallas_call | solution.py:289
  164.4 17.2 %all_to_all.36 = f32[32,8,256]{2,1,0:T(8,128)S(1)} all-to-all(f32[32,8,256]{2,1,0:T(8,128)} %partial_gram.1), channel_id=1, replica_groups=mesh['space'=4,'block'=8] {'space','block'}, dimensions={0} | all-to-all | bytes 524288 | tf_op jit(solution)/shard_map/all_to_all | solution.py:463
  181.7 13.0 %all_to_all.37 = f32[32,8,256]{2,1,0:T(8,128)} all-to-all(f32[32,8,256]{2,1,0:T(8,128)S(1)} %broadcast_in_dim.2), channel_id=1, replica_groups=mesh['space'=4,'block'=8] {'space','block'}, dimensions={0} | all-to-all | bytes 524288 | tf_op jit(solution)/shard_map/all_to_all | solution.py:464
  194.6 10.2 %inverse_factor.1.inverse = f32[256,256]{1,0:T(8,128)} custom-call(f32[256,256]{1,0:T(8,128)} %bitcast.5), custom_call_target="tpu_custom_call" | custom-call | tf_op jit(solution)/shard_map/inverse_factor/pallas_call | solution.py:422
  204.8 6.3 %product.1 = f32[8,32,4608]{2,1,0:T(8,128)} custom-call(f32[256,256]{1,0:T(8,128)} %inverse_factor.1.inverse, f32[8,8,4608]{2,1,0:T(8,128)} %copy-done, f32[8,8,4608]{2,1,0:T(8,128)} %copy-done.2, f32[8,8,4608]{2,1,0:T(8,128)} %all_to_all.35.refs_2_, f32[8,8,4608]{2,1,0:T(8,128)} %copy-done.1), custom_call_target="tpu_custom_call" | custom-call | tf_op jit(solution)/shard_map/product/pallas_call | solution.py:318
  211.2 59.2 %all_to_all.38 = f32[8,32,4608]{2,1,0:T(8,128)} all-to-all(f32[8,32,4608]{2,1,0:T(8,128)} %product.1), channel_id=1, replica_groups=mesh['space'=4,'block'=8] {'block'}, dimensions={0} | all-to-all | bytes 9437184 | tf_op jit(solution)/shard_map/all_to_all | solution.py:469
  270.3 4.3 %assemble.1 = f32[32,4,9216]{2,1,0:T(4,128)} custom-call(f32[4,2,32,4608]{3,2,1,0:T(8,128)} %bitcast.4), custom_call_target="tpu_custom_call" | custom-call | tf_op jit(solution)/shard_map/assemble/pallas_call | solution.py:338
  (28 shorter events, 9.7 us)
Async XLA Ops:
  2.5 18.3 %copy-start.5 = (f32[3]{0:T(128)S(1)}, f32[3]{0:T(128)}, u32[]{:S(2)}) copy-start(f32[3]{0:T(128)} %table.1) | copy-start | bytes 40
  2.5 35.3 %collective-permute-start.1 = (f32[9,4,9216]{2,1,0:T(4,128)}, f32[9,4,9216]{2,1,0:T(4,128)}, u32[]{:S(2)}, u32[]{:S(2)}) collective-permute-start(f32[9,4,9216]{2,1,0:T(4,128)} %first_chunk.1.own), channel_id=1, source_target_pairs={{8,0},{16,8},{24,16},{9,1},{17,9},{25,17},{10,2},{18,10},{26,18},{... | collective-permute-start | bytes 3981320 | tf_op jit(solution)/shard_map/ppermute | solution.py:455
  4.0 35.4 %collective-permute-start = (f32[9,4,9216]{2,1,0:T(4,128)}, f32[9,4,9216]{2,1,0:T(4,128)}, u32[]{:S(2)}, u32[]{:S(2)}) collective-permute-start(f32[9,4,9216]{2,1,0:T(4,128)} %first_chunk.1.own), channel_id=1, source_target_pairs={{0,8},{8,16},{16,24},{1,9},{9,17},{17,25},{2,10},{10,18},{18,26},{... | collective-permute-start | bytes 3981320 | tf_op jit(solution)/shard_map/ppermute | solution.py:454
  13.9 44.6 %copy-start.4 = (f32[8,4,9216]{2,1,0:T(4,128)}, f32[8,4,9216]{2,1,0:T(4,128)S(1)}, u32[]{:S(2)}) copy-start(f32[8,4,9216]{2,1,0:T(4,128)S(1)} %get-tuple-element.9.own) | copy-start | bytes 3538948
  13.9 77.5 %copy-start.3 = (f32[8,4,9216]{2,1,0:T(4,128)}, f32[8,4,9216]{2,1,0:T(4,128)S(1)}, u32[]{:S(2)}) copy-start(f32[8,4,9216]{2,1,0:T(4,128)S(1)} %get-tuple-element.11.own) | copy-start | bytes 3538948
  13.9 56.1 %collective-permute-start.7 = (f32[8,4,9216]{2,1,0:T(4,128)S(1)}, f32[8,4,9216]{2,1,0:T(4,128)}, u32[]{:S(2)}, u32[]{:S(2)}) collective-permute-start(f32[8,4,9216]{2,1,0:T(4,128)S(1)} %get-tuple-element.9.own), channel_id=1, source_target_pairs={{8,0},{16,8},{24,16},{9,1},{17,9},{25,17},{10,2},{18,10},{26,18},{... | collective-permute-start | bytes 3538952 | tf_op jit(solution)/shard_map/ppermute | solution.py:455
  15.2 54.9 %collective-permute-start.6 = (f32[8,4,9216]{2,1,0:T(4,128)S(1)}, f32[8,4,9216]{2,1,0:T(4,128)}, u32[]{:S(2)}, u32[]{:S(2)}) collective-permute-start(f32[8,4,9216]{2,1,0:T(4,128)S(1)} %get-tuple-element.9.own), channel_id=1, source_target_pairs={{0,8},{8,16},{16,24},{1,9},{9,17},{17,25},{2,10},{10,18},{18,26},{... | collective-permute-start | bytes 3538952 | tf_op jit(solution)/shard_map/ppermute | solution.py:454
  58.5 26.4 %all-to-all-start = ((f32[8,8,4608]{2,1,0:T(8,128)}), f32[8,8,4608]{2,1,0:T(8,128)S(1)}, u32[]{:S(2)}, u32[]{:S(2)}) async-start(f32[8,8,4608]{2,1,0:T(8,128)} %get-tuple-element.7), calls=%async_computation | async-start | bytes 2359296 | tf_op jit(solution)/shard_map/all_to_all | solution.py:460
  62.7 34.3 %collective-permute-start.3 = (f32[8,4,9216]{2,1,0:T(4,128)}, f32[8,4,9216]{2,1,0:T(4,128)}, u32[]{:S(2)}, u32[]{:S(2)}) collective-permute-start(f32[8,4,9216]{2,1,0:T(4,128)} %get-tuple-element.10.own), channel_id=1, source_target_pairs={{8,0},{16,8},{24,16},{9,1},{17,9},{25,17},{10,2},{18,10},{26,18},{... | collective-permute-start | bytes 3538952 | tf_op jit(solution)/shard_map/ppermute | solution.py:455
  64.0 33.0 %collective-permute-start.2 = (f32[8,4,9216]{2,1,0:T(4,128)}, f32[8,4,9216]{2,1,0:T(4,128)}, u32[]{:S(2)}, u32[]{:S(2)}) collective-permute-start(f32[8,4,9216]{2,1,0:T(4,128)} %get-tuple-element.10.own), channel_id=1, source_target_pairs={{0,8},{8,16},{16,24},{1,9},{9,17},{17,25},{2,10},{10,18},{18,26},{... | collective-permute-start | bytes 3538952 | tf_op jit(solution)/shard_map/ppermute | solution.py:454
  84.9 1.0 copy-start
  85.9 25.9 %all-to-all-start.3 = ((f32[8,8,4608]{2,1,0:T(8,128)}), f32[8,8,4608]{2,1,0:T(8,128)S(1)}, u32[]{:S(2)}, u32[]{:S(2)}) async-start(f32[8,8,4608]{2,1,0:T(8,128)} %chebyshev.5), calls=%async_computation.3 | async-start | bytes 2359296 | tf_op jit(solution)/shard_map/all_to_all | solution.py:460
  90.1 30.4 %collective-permute-start.5 = (f32[8,4,9216]{2,1,0:T(4,128)S(1)}, f32[8,4,9216]{2,1,0:T(4,128)}, u32[]{:S(2)}, u32[]{:S(2)}) collective-permute-start(f32[8,4,9216]{2,1,0:T(4,128)S(1)} %get-tuple-element.11.own), channel_id=1, source_target_pairs={{8,0},{16,8},{24,16},{9,1},{17,9},{25,17},{10,2},{18,10},{26,18},{... | collective-permute-start | bytes 3538952 | tf_op jit(solution)/shard_map/ppermute | solution.py:455
  91.4 30.2 %collective-permute-start.4 = (f32[8,4,9216]{2,1,0:T(4,128)S(1)}, f32[8,4,9216]{2,1,0:T(4,128)}, u32[]{:S(2)}, u32[]{:S(2)}) collective-permute-start(f32[8,4,9216]{2,1,0:T(4,128)S(1)} %get-tuple-element.11.own), channel_id=1, source_target_pairs={{0,8},{8,16},{16,24},{1,9},{9,17},{17,25},{2,10},{10,18},{18,26},{... | collective-permute-start | bytes 3538952 | tf_op jit(solution)/shard_map/ppermute | solution.py:454
  111.8 1.0 copy-start.1
  112.8 23.5 %all-to-all-start.1 = ((f32[8,8,4608]{2,1,0:T(8,128)}), f32[8,8,4608]{2,1,0:T(8,128)S(1)}, u32[]{:S(2)}, u32[]{:S(2)}) async-start(f32[8,8,4608]{2,1,0:T(8,128)} %chebyshev.3), calls=%async_computation.1 | async-start | bytes 2359296 | tf_op jit(solution)/shard_map/all_to_all | solution.py:460
  136.4 21.0 %copy-start.2 = (f32[8,8,4608]{2,1,0:T(8,128)}, f32[8,8,4608]{2,1,0:T(8,128)S(1)}, u32[]{:S(2)}) copy-start(f32[8,8,4608]{2,1,0:T(8,128)S(1)} %all-to-all-done.1.refs_1_) | copy-start | bytes 3538948

commit v3 on v2

--- a/solution.py
+++ b/solution.py
@@ -13,7 +13,7 @@
 LANES = 128
 CHUNK = 8
 PANEL = 64
-BLOCK = 9 * LANES
+BLOCK = 18 * LANES
 HIGHEST = lax.Precision.HIGHEST
 
 
@@ -110,14 +110,17 @@
     return copies
 
 
-def filter_kernel(planes, halves, raw, terms, target_array, out, sems, y0, y1, y2, y3):
+def filter_kernel(planes, halves, arriving, raw, terms, target_array, out, sems, y0, y1, y2, y3):
     for k in range(3):
+        if k < len(arriving):
+            arriving[k].wait()
         for p in range(planes):
             y0[k * planes + p] = raw[k, 0:CHUNK, p, :]
+    for copy in arriving[3:]:
+        copy.wait()
     cells = y0.shape[-1]
     tiles = cells // LANES
     per_half = tiles // halves
-    group = per_half
     lane = lax.broadcasted_iota(jnp.int32, (CHUNK, LANES), 1)
     last, first = lane == LANES - 1, lane == 0
     head, tail = lane < NZ, lane >= LANES - NZ
@@ -128,45 +131,30 @@
         def plane_body(p, carry):
             w = p + at
 
-            def group_body(g, carry):
-                t0 = g * group
-                s = source_at(w)
-                span = pl.ds(pl.multiple_of(t0 * LANES, LANES), group * LANES)
-                before = jnp.where(t0 == 0, tiles - 1, t0 - 1)
-                after = jnp.where(t0 + group == tiles, 0, t0 + group)
-
-                def edge(t):
-                    return source[s, :, pl.ds(pl.multiple_of(t * LANES, LANES), LANES)]
-
-                def cut(wide):
-                    return [wide[:, i * LANES : (i + 1) * LANES] for i in range(group)]
-
-                row = [edge(before)] + cut(source[s, :, span]) + [edge(after)]
-                below, above = cut(source[s - 1, :, span]), cut(source[s + 1, :, span])
-                rows = [cut(terms[w - 1, pl.ds(k, 1), span]) for k in range(7)]
-                if not half_step:
-                    older = cut(previous[previous_at(w), :, span])
-                results = []
-                for i in range(group):
-                    left, here, right = row[i : i + 3]
-                    total = rows[0][i] * here
-                    total += rows[1][i] * below[i]
-                    total += rows[2][i] * above[i]
-                    total += rows[3][i] * pltpu.roll(jnp.where(first, right, here), LANES - 1, 1)
-                    total += rows[4][i] * pltpu.roll(jnp.where(last, left, here), 1, 1)
-                    total += rows[5][i] * pltpu.roll(jnp.where(head, right, here), LANES - NZ, 1)
-                    total += rows[6][i] * pltpu.roll(jnp.where(tail, left, here), NZ, 1)
-                    results.append(0.5 * total if half_step else total - older[i])
-                result = jnp.concatenate(results, axis=1)
+            s = source_at(w)
+
+            def tile(array, plane, t):
+                return array[plane, :, t * LANES : (t + 1) * LANES]
+
+            row = [tile(source, s, tiles - 1), tile(source, s, 0)]
+            for t in range(tiles):
+                left, here = row
+                right = tile(source, s, (t + 1) % tiles)
+                row = [here, right]
+                term = [terms[w - 1, k : k + 1, t * LANES : (t + 1) * LANES] for k in range(7)]
+                total = term[0] * here
+                total += term[1] * tile(source, s - 1, t)
+                total += term[2] * tile(source, s + 1, t)
+                total += term[3] * pltpu.roll(jnp.where(first, right, here), LANES - 1, 1)
+                total += term[4] * pltpu.roll(jnp.where(last, left, here), 1, 1)
+                total += term[5] * pltpu.roll(jnp.where(head, right, here), LANES - NZ, 1)
+                total += term[6] * pltpu.roll(jnp.where(tail, left, here), NZ, 1)
+                total = 0.5 * total if half_step else total - tile(previous, previous_at(w), t)
                 if target is out:
-                    half = lax.div(t0, per_half)
-                    inner = pl.multiple_of((t0 - half * per_half) * LANES, LANES)
-                    out[p * halves + half, :, pl.ds(inner, group * LANES)] = result
+                    inner = t % per_half * LANES
+                    out[p * halves + t // per_half, :, inner : inner + LANES] = total
                 else:
-                    target[p, :, span] = result
-                return carry
-
-            lax.fori_loop(0, tiles // group, group_body, 0, unroll=True)
+                    target[p, :, t * LANES : (t + 1) * LANES] = total
             if target is out:
                 leaving(p).start()
             return carry
@@ -194,11 +182,8 @@
     copies = start_reading((low, own, high), raw, sems)
     last = pltpu.make_async_copy(stored, terms, sems.at[3 + planes])
     last.start()
-    for copy in copies:
-        copy.wait()
-    last.wait()
     filter_kernel(
-        planes, halves, raw, terms, target, out, sems.at[pl.ds(3, planes)], y0, y1, y2, y3
+        planes, halves, (*copies, last), raw, terms, target, out, sems.at[pl.ds(3, planes)], y0, y1, y2, y3
     )
 
 
@@ -211,7 +196,7 @@
     last = pltpu.make_async_copy(terms, stored, sems.at[3 + planes])
     last.start()
     filter_kernel(
-        planes, halves, raw, terms, target, out, sems.at[pl.ds(3, planes)], y0, y1, y2, y3
+        planes, halves, (), raw, terms, target, out, sems.at[pl.ds(3, planes)], y0, y1, y2, y3
     )
     last.wait()
 
@@ -265,21 +250,42 @@
     return jnp.concatenate([c[b] for b in range(blocks) for c in chunks], axis=0)
 
 
+def halved(value):
+    high = value.astype(jnp.bfloat16)
+    return high, (value - high.astype(jnp.float32)).astype(jnp.bfloat16)
+
+
+def dot(left, right):
+    return jnp.dot(left, right, preferred_element_type=jnp.float32)
+
+
 def gram_kernel(*refs):
-    *chunks, out = refs
-    field = rows_in_order(chunks)
-    update = lax.dot_general(
-        field, field, (((1,), (1,)), ((), ())), precision=HIGHEST,
-        preferred_element_type=jnp.float32,
-    ).reshape(out.shape)
-
-    @pl.when(pl.program_id(0) == 0)
+    *chunks, out, cross = refs
+    step = pl.program_id(0)
+    rank = cross.shape[0]
+    high, low = halved(rows_in_order(chunks))
+
+    def inner(left, right):
+        return lax.dot_general(
+            left, right, (((1,), (1,)), ((), ())), preferred_element_type=jnp.float32
+        )
+
+    square, mixed = inner(high, high).reshape(out.shape), inner(high, low)
+
+    @pl.when(step == 0)
     def _():
-        out[...] = update
-
-    @pl.when(pl.program_id(0) > 0)
+        out[...] = square
+        cross[...] = mixed
+
+    @pl.when(step > 0)
     def _():
-        out[...] += update
+        out[...] += square
+        cross[...] += mixed
+
+    @pl.when(step == pl.num_programs(0) - 1)
+    def _():
+        both = cross[...] + jnp.transpose(cross[...])
+        out[...] += both.reshape(out.shape)
 
 
 def partial_gram(chunks, pieces):
@@ -292,18 +298,10 @@
         out_shape=jax.ShapeDtypeStruct(shape, jnp.float32),
         in_specs=[pl.BlockSpec((blocks, rows, BLOCK), lambda i: (0, 0, i))] * len(chunks),
         out_specs=pl.BlockSpec(shape, lambda i: (0, 0, 0)),
+        scratch_shapes=[pltpu.VMEM((rank, rank), jnp.float32)],
         compiler_params=pltpu.CompilerParams(vmem_limit_bytes=60 * 2**20),
         name="partial_gram",
     )(*chunks)
-
-
-def halved(value):
-    high = value.astype(jnp.bfloat16)
-    return high, (value - high.astype(jnp.float32)).astype(jnp.bfloat16)
-
-
-def dot(left, right):
-    return jnp.dot(left, right, preferred_element_type=jnp.float32)
 
 
 def product_kernel(inverse, *refs):
@@ -341,7 +339,7 @@
         out_shape=jax.ShapeDtypeStruct((rows, planes, halves * width), jnp.float32),
         in_specs=[pl.BlockSpec((planes, 1, rows, width), lambda i: (0, i, 0, 0))],
         out_specs=pl.BlockSpec((rows, planes, width), lambda i: (0, 0, i)),
-        compiler_params=pltpu.CompilerParams(vmem_limit_bytes=60 * 2**20),
+        compiler_params=pltpu.CompilerParams(vmem_limit_bytes=32 * 2**20),
         name="assemble",
     )(pieces)
 
@@ -453,11 +451,17 @@
             own = start_vectors[c * CHUNK : (c + 1) * CHUNK]
         low = lax.ppermute(own, "space", up)
         high = lax.ppermute(own, "space", back)
+        if c >= 1:
+            low, high, part = lax.optimization_barrier((low, high, part))
+            if received:
+                part, received[-1] = lax.optimization_barrier((part, received[-1]))
+            received.append(lax.all_to_all(part, "block", 0, 0, tiled=True))
         if c == 0:
             part, terms = filtered(low, own, high, blocks, scales=scales)
         else:
             part = filtered(low, own, high, blocks, terms=terms)
-        received.append(lax.all_to_all(part, "block", 0, 0, tiled=True))
+    part, received[-1] = lax.optimization_barrier((part, received[-1]))
+    received.append(lax.all_to_all(part, "block", 0, 0, tiled=True))
     devices = blocks * slabs
     pieces = partial_gram(received, devices)
     summed = jnp.sum(lax.all_to_all(pieces, ("space", "block"), 0, 0, tiled=True), axis=0)

time: 276 us -> 268 us (0.971)
  waiting for transfers between devices: 20.5 us -> 30.4 us
  Pallas kernels: 93.8 us -> 87.4 us
  blocking collectives: 110 us -> 105 us
  starting transfers between devices: 41.8 us -> 37.1 us
    ppermute x4, waiting for transfers between devices: 2.59 us -> 13.2 us  [local(): low = lax.ppermute(own, 'space', up)]
    all_to_all x1, blocking collectives: 17.2 us -> 13.2 us  [local(): lax.all_to_all(pieces, ('space', 'block'), 0, 0, tiled=True)]
    ppermute x4, waiting for transfers between devices: 17.9 us -> 14.6 us  [local(): high = lax.ppermute(own, 'space', back)]
    ppermute x4, starting transfers between devices: 24 us -> 20.8 us  [local(): low = lax.ppermute(own, 'space', up)]
    pallas_call x1, Pallas kernels: 6.98 us -> 4.17 us  [partial_gram(): pl.pallas_call(gram_kernel, grid=(width // BLOCK,), out_shape=jax.ShapeDt...]
  transfers between devices with their start and end apart: 11 -> 11, of which waited for: 4 -> 7; matrix products, arithmetic and copies ran while one was open for 2% -> 1% of each run, Pallas kernels for 23% -> 23%
where the time goes in v3:
time: 268 us
  blocking collectives  105 us (39%)
  Pallas kernels  87.4 us (33%)
  starting transfers between devices  37.1 us (14%)
  waiting for transfers between devices  30.4 us (11%)
  local copies, waits for them, and re-layouts  4.33 us (2%)
    all_to_all x1, blocking collectives, local(): sent = lax.all_to_all(result, 'block', 0, 0, tiled=True)  58.3 us
    pallas_call x3, Pallas kernels, filtered(): pl.pallas_call(functools.partial(next_filter_kernel, planes, halves), out...  42.6 us
    all_to_all x1, blocking collectives, local(): received.append(lax.all_to_all(part, 'block', 0, 0, tiled=True))  21 us
    ppermute x4, starting transfers between devices, local(): low = lax.ppermute(own, 'space', up)  20.8 us
    pallas_call x1, Pallas kernels, filtered(): pl.pallas_call(functools.partial(first_filter_kernel, planes, halves), ou...  19.2 us
    ppermute x4, waiting for transfers between devices, local(): high = lax.ppermute(own, 'space', back)  14.6 us
    ppermute x4, waiting for transfers between devices, local(): low = lax.ppermute(own, 'space', up)  13.2 us
    all_to_all x1, blocking collectives, local(): lax.all_to_all(pieces, ('space', 'block'), 0, 0, tiled=True)  13.2 us
  transfers between devices with their start and end apart: 11, of which 7 were waited for; matrix products, arithmetic and copies ran while one was open for 1% of the time, Pallas kernels for 23%

profile of v3, /device:TPU:0, one launch (start us, length us, event | category | flops | bytes accessed | tf_op | source)
XLA Modules:
  0.0 267.5 jit_solution(14898040839085477614)
XLA Ops:
  0.0 2.6 first_chunk.1.own
  2.6 6.1 %collective-permute-start.4 = (f32[9,4,9216]{2,1,0:T(4,128)}, f32[9,4,9216]{2,1,0:T(4,128)}, u32[]{:S(2)}, u32[]{:S(2)}) collective-permute-start(f32[9,4,9216]{2,1,0:T(4,128)} %first_chunk.1.own), channel_id=1, source_target_pairs={{0,8},{8,16},{16,24},{1,9},{9,17},{17,25},{2,10},{10,18},{18,26},{... | collective-permute-start | bytes 3981320 | tf_op jit(solution)/shard_map/ppermute | solution.py:452
  12.3 5.6 %collective-permute-start.2 = (f32[8,4,9216]{2,1,0:T(4,128)S(1)}, f32[8,4,9216]{2,1,0:T(4,128)}, u32[]{:S(2)}, u32[]{:S(2)}) collective-permute-start(f32[8,4,9216]{2,1,0:T(4,128)S(1)} %get-tuple-element.40.own), channel_id=1, source_target_pairs={{0,8},{8,16},{16,24},{1,9},{9,17},{17,25},{2,10},{10,18},{18,26},{... | collective-permute-start | bytes 3538952 | tf_op jit(solution)/shard_map/ppermute | solution.py:452
  19.2 5.6 %collective-permute-start = (f32[8,4,9216]{2,1,0:T(4,128)S(1)}, f32[8,4,9216]{2,1,0:T(4,128)}, u32[]{:S(2)}, u32[]{:S(2)}) collective-permute-start(f32[8,4,9216]{2,1,0:T(4,128)S(1)} %get-tuple-element.41.own), channel_id=1, source_target_pairs={{0,8},{8,16},{16,24},{1,9},{9,17},{17,25},{2,10},{10,18},{18,26},{... | collective-permute-start | bytes 3538952 | tf_op jit(solution)/shard_map/ppermute | solution.py:452
  24.8 12.7 %collective-permute-done.4.low = f32[9,4,9216]{2,1,0:T(4,128)} collective-permute-done((f32[9,4,9216]{2,1,0:T(4,128)}, f32[9,4,9216]{2,1,0:T(4,128)}, u32[]{:S(2)}, u32[]{:S(2)}) %collective-permute-start.4) | collective-permute-done | bytes 1327136 | tf_op jit(solution)/shard_map/ppermute | solution.py:452
  43.0 19.2 %first_chebyshev.1 = (f32[8,8,4608]{2,1,0:T(8,128)}, f32[10,8,9216]{2,1,0:T(8,128)}) custom-call(f32[2]{0:T(128)} %pad_maximum_fusion.scales, f32[9,4,9216]{2,1,0:T(4,128)} %collective-permute-done.4.low, f32[9,4,9216]{2,1,0:T(4,128)} %first_chunk.1.own, f32[9,4,9216]{2,1,0:T(4,128)} %collective-permute-done.5.high), custom_call_target="tpu_custom_call" | custom-call | flops 28901376 | bytes 12976128 | tf_op jit(solution)/shard_map/first_chebyshev/pallas_call | solution.py:237
  62.7 5.6 %collective-permute-done.3.high = f32[8,4,9216]{2,1,0:T(4,128)} collective-permute-done((f32[8,4,9216]{2,1,0:T(4,128)S(1)}, f32[8,4,9216]{2,1,0:T(4,128)}, u32[]{:S(2)}, u32[]{:S(2)}) %collective-permute-start.3) | collective-permute-done | bytes 1179680 | tf_op jit(solution)/shard_map/ppermute | solution.py:453
  68.3 3.7 %all-to-all-start = ((f32[8,8,4608]{2,1,0:T(8,128)}), f32[8,8,4608]{2,1,0:T(8,128)S(1)}, u32[]{:S(2)}, u32[]{:S(2)}) async-start(f32[8,8,4608]{2,1,0:T(8,128)} %get-tuple-element.27), calls=%async_computation | async-start | bytes 2359296 | tf_op jit(solution)/shard_map/all_to_all | solution.py:458
  72.0 3.5 %collective-permute-start.6 = (f32[8,4,9216]{2,1,0:T(4,128)S(1)}, f32[8,4,9216]{2,1,0:T(4,128)}, u32[]{:S(2)}, u32[]{:S(2)}) collective-permute-start(f32[8,4,9216]{2,1,0:T(4,128)S(1)} %get-tuple-element.39.own), channel_id=1, source_target_pairs={{0,8},{8,16},{16,24},{1,9},{9,17},{17,25},{2,10},{10,18},{18,26},{... | collective-permute-start | bytes 3538952 | tf_op jit(solution)/shard_map/ppermute | solution.py:452
  76.8 14.2 %chebyshev.3 = f32[8,8,4608]{2,1,0:T(8,128)} custom-call(f32[8,4,9216]{2,1,0:T(4,128)} %collective-permute-done.2.low, f32[8,4,9216]{2,1,0:T(4,128)} %copy-done.5, f32[8,4,9216]{2,1,0:T(4,128)} %collective-permute-done.3.high, f32[10,8,9216]{2,1,0:T(8,128)} %get-tuple-element.25.stored), custom_call_target="tpu_custom_call" | custom-call | flops 28901376 | bytes 12976128 | tf_op jit(solution)/shard_map/chebyshev/pallas_call | solution.py:228
  94.6 3.7 %all-to-all-start.1 = ((f32[8,8,4608]{2,1,0:T(8,128)}), f32[8,8,4608]{2,1,0:T(8,128)S(1)}, u32[]{:S(2)}, u32[]{:S(2)}) async-start(f32[8,8,4608]{2,1,0:T(8,128)} %chebyshev.3), calls=%async_computation.1 | async-start | bytes 2359296 | tf_op jit(solution)/shard_map/all_to_all | solution.py:458
  98.3 14.2 %chebyshev.4 = f32[8,8,4608]{2,1,0:T(8,128)} custom-call(f32[8,4,9216]{2,1,0:T(4,128)} %collective-permute-done.low, f32[8,4,9216]{2,1,0:T(4,128)} %copy-done.4, f32[8,4,9216]{2,1,0:T(4,128)} %collective-permute-done.1.high, f32[10,8,9216]{2,1,0:T(8,128)} %get-tuple-element.25.stored), custom_call_target="tpu_custom_call" | custom-call | flops 28901376 | bytes 12976128 | tf_op jit(solution)/shard_map/chebyshev/pallas_call | solution.py:228
  112.6 4.8 %collective-permute-done.7.high = f32[8,4,9216]{2,1,0:T(4,128)} collective-permute-done((f32[8,4,9216]{2,1,0:T(4,128)S(1)}, f32[8,4,9216]{2,1,0:T(4,128)}, u32[]{:S(2)}, u32[]{:S(2)}) %collective-permute-start.7) | collective-permute-done | bytes 1179680 | tf_op jit(solution)/shard_map/ppermute | solution.py:453
  118.4 3.7 %all-to-all-start.2 = ((f32[8,8,4608]{2,1,0:T(8,128)}), f32[8,8,4608]{2,1,0:T(8,128)S(1)}, u32[]{:S(2)}, u32[]{:S(2)}) async-start(f32[8,8,4608]{2,1,0:T(8,128)} %chebyshev.4), calls=%async_computation.2 | async-start | bytes 2359296 | tf_op jit(solution)/shard_map/all_to_all | solution.py:458
  122.2 14.2 %chebyshev.5 = f32[8,8,4608]{2,1,0:T(8,128)} custom-call(f32[8,4,9216]{2,1,0:T(4,128)} %collective-permute-done.6.low, f32[8,4,9216]{2,1,0:T(4,128)} %copy-done.3, f32[8,4,9216]{2,1,0:T(4,128)} %collective-permute-done.7.high, f32[10,8,9216]{2,1,0:T(8,128)} %get-tuple-element.25.stored), custom_call_target="tpu_custom_call" | custom-call | flops 28901376 | bytes 12976128 | tf_op jit(solution)/shard_map/chebyshev/pallas_call | solution.py:228
  136.3 2.6 all-to-all-done.2.refs_2_
  139.0 21.0 %all_to_all.35.refs_3_ = f32[8,8,4608]{2,1,0:T(8,128)} all-to-all(f32[8,8,4608]{2,1,0:T(8,128)} %chebyshev.5), channel_id=1, replica_groups=mesh['space'=4,'block'=8] {'block'}, dimensions={0} | all-to-all | bytes 2359296 | tf_op jit(solution)/shard_map/all_to_all | solution.py:464
  160.0 4.2 %partial_gram.1 = f32[32,8,256]{2,1,0:T(8,128)} custom-call(f32[8,8,4608]{2,1,0:T(8,128)} %copy-done, f32[8,8,4608]{2,1,0:T(8,128)} %copy-done.1, f32[8,8,4608]{2,1,0:T(8,128)} %copy-done.2, f32[8,8,4608]{2,1,0:T(8,128)} %all_to_all.35.refs_3_), custom_call_target="tpu_custom_call" | custom-call | tf_op jit(solution)/shard_map/partial_gram/pallas_call | solution.py:295
  164.2 13.2 %all_to_all.36 = f32[32,8,256]{2,1,0:T(8,128)S(1)} all-to-all(f32[32,8,256]{2,1,0:T(8,128)} %partial_gram.1), channel_id=1, replica_groups=mesh['space'=4,'block'=8] {'space','block'}, dimensions={0} | all-to-all | bytes 524288 | tf_op jit(solution)/shard_map/all_to_all | solution.py:467
  177.4 13.0 %all_to_all.37 = f32[32,8,256]{2,1,0:T(8,128)} all-to-all(f32[32,8,256]{2,1,0:T(8,128)S(1)} %broadcast_in_dim.2), channel_id=1, replica_groups=mesh['space'=4,'block'=8] {'space','block'}, dimensions={0} | all-to-all | bytes 524288 | tf_op jit(solution)/shard_map/all_to_all | solution.py:468
  190.4 10.2 %inverse_factor.1.inverse = f32[256,256]{1,0:T(8,128)} custom-call(f32[256,256]{1,0:T(8,128)} %bitcast.5), custom_call_target="tpu_custom_call" | custom-call | tf_op jit(solution)/shard_map/inverse_factor/pallas_call | solution.py:420
  200.6 5.7 %product.1 = f32[8,32,4608]{2,1,0:T(8,128)} custom-call(f32[256,256]{1,0:T(8,128)} %inverse_factor.1.inverse, f32[8,8,4608]{2,1,0:T(8,128)} %copy-done, f32[8,8,4608]{2,1,0:T(8,128)} %copy-done.1, f32[8,8,4608]{2,1,0:T(8,128)} %copy-done.2, f32[8,8,4608]{2,1,0:T(8,128)} %all_to_all.35.refs_3_), custom_call_target="tpu_custom_call" | custom-call | tf_op jit(solution)/shard_map/product/pallas_call | solution.py:316
  206.2 58.3 %all_to_all.38 = f32[8,32,4608]{2,1,0:T(8,128)S(1)} all-to-all(f32[8,32,4608]{2,1,0:T(8,128)} %product.1), channel_id=1, replica_groups=mesh['space'=4,'block'=8] {'block'}, dimensions={0} | all-to-all | bytes 9437184 | tf_op jit(solution)/shard_map/all_to_all | solution.py:473
  264.5 3.0 %assemble.1 = f32[32,4,9216]{2,1,0:T(4,128)} custom-call(f32[4,2,32,4608]{3,2,1,0:T(8,128)S(1)} %bitcast.4), custom_call_target="tpu_custom_call" | custom-call | tf_op jit(solution)/shard_map/assemble/pallas_call | solution.py:336
  (30 shorter events, 15.4 us)
Async XLA Ops:
  2.6 36.2 %copy-start.6 = (f32[3]{0:T(128)S(1)}, f32[3]{0:T(128)}, u32[]{:S(2)}) copy-start(f32[3]{0:T(128)} %table.1) | copy-start | bytes 40
  2.6 34.9 %collective-permute-start.4 = (f32[9,4,9216]{2,1,0:T(4,128)}, f32[9,4,9216]{2,1,0:T(4,128)}, u32[]{:S(2)}, u32[]{:S(2)}) collective-permute-start(f32[9,4,9216]{2,1,0:T(4,128)} %first_chunk.1.own), channel_id=1, source_target_pairs={{0,8},{8,16},{16,24},{1,9},{9,17},{17,25},{2,10},{10,18},{18,26},{... | collective-permute-start | bytes 3981320 | tf_op jit(solution)/shard_map/ppermute | solution.py:452
  8.8 34.3 %collective-permute-start.5 = (f32[9,4,9216]{2,1,0:T(4,128)}, f32[9,4,9216]{2,1,0:T(4,128)}, u32[]{:S(2)}, u32[]{:S(2)}) collective-permute-start(f32[9,4,9216]{2,1,0:T(4,128)} %first_chunk.1.own), channel_id=1, source_target_pairs={{8,0},{16,8},{24,16},{9,1},{17,9},{25,17},{10,2},{18,10},{26,18},{... | collective-permute-start | bytes 3981320 | tf_op jit(solution)/shard_map/ppermute | solution.py:453
  12.3 49.9 %copy-start.4 = (f32[8,4,9216]{2,1,0:T(4,128)}, f32[8,4,9216]{2,1,0:T(4,128)S(1)}, u32[]{:S(2)}) copy-start(f32[8,4,9216]{2,1,0:T(4,128)S(1)} %get-tuple-element.41.own) | copy-start | bytes 3538948
  12.3 49.9 %copy-start.5 = (f32[8,4,9216]{2,1,0:T(4,128)}, f32[8,4,9216]{2,1,0:T(4,128)S(1)}, u32[]{:S(2)}) copy-start(f32[8,4,9216]{2,1,0:T(4,128)S(1)} %get-tuple-element.40.own) | copy-start | bytes 3538948
  12.3 63.2 %copy-start.3 = (f32[8,4,9216]{2,1,0:T(4,128)}, f32[8,4,9216]{2,1,0:T(4,128)S(1)}, u32[]{:S(2)}) copy-start(f32[8,4,9216]{2,1,0:T(4,128)S(1)} %get-tuple-element.39.own) | copy-start | bytes 3538948
  12.3 50.4 %collective-permute-start.2 = (f32[8,4,9216]{2,1,0:T(4,128)S(1)}, f32[8,4,9216]{2,1,0:T(4,128)}, u32[]{:S(2)}, u32[]{:S(2)}) collective-permute-start(f32[8,4,9216]{2,1,0:T(4,128)S(1)} %get-tuple-element.40.own), channel_id=1, source_target_pairs={{0,8},{8,16},{16,24},{1,9},{9,17},{17,25},{2,10},{10,18},{18,26},{... | collective-permute-start | bytes 3538952 | tf_op jit(solution)/shard_map/ppermute | solution.py:452
  17.9 50.4 %collective-permute-start.3 = (f32[8,4,9216]{2,1,0:T(4,128)S(1)}, f32[8,4,9216]{2,1,0:T(4,128)}, u32[]{:S(2)}, u32[]{:S(2)}) collective-permute-start(f32[8,4,9216]{2,1,0:T(4,128)S(1)} %get-tuple-element.40.own), channel_id=1, source_target_pairs={{8,0},{16,8},{24,16},{9,1},{17,9},{25,17},{10,2},{18,10},{26,18},{... | collective-permute-start | bytes 3538952 | tf_op jit(solution)/shard_map/ppermute | solution.py:453
  19.2 71.8 %collective-permute-start = (f32[8,4,9216]{2,1,0:T(4,128)S(1)}, f32[8,4,9216]{2,1,0:T(4,128)}, u32[]{:S(2)}, u32[]{:S(2)}) collective-permute-start(f32[8,4,9216]{2,1,0:T(4,128)S(1)} %get-tuple-element.41.own), channel_id=1, source_target_pairs={{0,8},{8,16},{16,24},{1,9},{9,17},{17,25},{2,10},{10,18},{18,26},{... | collective-permute-start | bytes 3538952 | tf_op jit(solution)/shard_map/ppermute | solution.py:452
  37.5 56.1 %collective-permute-start.1 = (f32[8,4,9216]{2,1,0:T(4,128)S(1)}, f32[8,4,9216]{2,1,0:T(4,128)}, u32[]{:S(2)}, u32[]{:S(2)}) collective-permute-start(f32[8,4,9216]{2,1,0:T(4,128)S(1)} %get-tuple-element.41.own), channel_id=1, source_target_pairs={{8,0},{16,8},{24,16},{9,1},{17,9},{25,17},{10,2},{18,10},{26,18},{... | collective-permute-start | bytes 3538952 | tf_op jit(solution)/shard_map/ppermute | solution.py:453
  68.3 25.3 %all-to-all-start = ((f32[8,8,4608]{2,1,0:T(8,128)}), f32[8,8,4608]{2,1,0:T(8,128)S(1)}, u32[]{:S(2)}, u32[]{:S(2)}) async-start(f32[8,8,4608]{2,1,0:T(8,128)} %get-tuple-element.27), calls=%async_computation | async-start | bytes 2359296 | tf_op jit(solution)/shard_map/all_to_all | solution.py:458
  72.0 40.6 %collective-permute-start.6 = (f32[8,4,9216]{2,1,0:T(4,128)S(1)}, f32[8,4,9216]{2,1,0:T(4,128)}, u32[]{:S(2)}, u32[]{:S(2)}) collective-permute-start(f32[8,4,9216]{2,1,0:T(4,128)S(1)} %get-tuple-element.39.own), channel_id=1, source_target_pairs={{0,8},{8,16},{16,24},{1,9},{9,17},{17,25},{2,10},{10,18},{18,26},{... | collective-permute-start | bytes 3538952 | tf_op jit(solution)/shard_map/ppermute | solution.py:452
  75.5 41.9 %collective-permute-start.7 = (f32[8,4,9216]{2,1,0:T(4,128)S(1)}, f32[8,4,9216]{2,1,0:T(4,128)}, u32[]{:S(2)}, u32[]{:S(2)}) collective-permute-start(f32[8,4,9216]{2,1,0:T(4,128)S(1)} %get-tuple-element.39.own), channel_id=1, source_target_pairs={{8,0},{16,8},{24,16},{9,1},{17,9},{25,17},{10,2},{18,10},{26,18},{... | collective-permute-start | bytes 3538952 | tf_op jit(solution)/shard_map/ppermute | solution.py:453
  93.6 1.0 copy-start
  94.6 22.8 %all-to-all-start.1 = ((f32[8,8,4608]{2,1,0:T(8,128)}), f32[8,8,4608]{2,1,0:T(8,128)S(1)}, u32[]{:S(2)}, u32[]{:S(2)}) async-start(f32[8,8,4608]{2,1,0:T(8,128)} %chebyshev.3), calls=%async_computation.1 | async-start | bytes 2359296 | tf_op jit(solution)/shard_map/all_to_all | solution.py:458
  117.4 1.0 copy-start.1
  118.4 20.5 %all-to-all-start.2 = ((f32[8,8,4608]{2,1,0:T(8,128)}), f32[8,8,4608]{2,1,0:T(8,128)S(1)}, u32[]{:S(2)}, u32[]{:S(2)}) async-start(f32[8,8,4608]{2,1,0:T(8,128)} %chebyshev.4), calls=%async_computation.2 | async-start | bytes 2359296 | tf_op jit(solution)/shard_map/all_to_all | solution.py:458
  139.0 21.0 %copy-start.2 = (f32[8,8,4608]{2,1,0:T(8,128)}, f32[8,8,4608]{2,1,0:T(8,128)S(1)}, u32[]{:S(2)}) copy-start(f32[8,8,4608]{2,1,0:T(8,128)S(1)} %all-to-all-done.2.refs_2_) | copy-start | bytes 3538948

commit v4 on v3

--- a/solution.py
+++ b/solution.py
@@ -101,6 +101,15 @@
     lax.fori_loop(0, cells // span, body, 0)
 
 
+def halved(value):
+    high = value.astype(jnp.bfloat16)
+    return high, (value - high.astype(jnp.float32)).astype(jnp.bfloat16)
+
+
+def dot(left, right):
+    return jnp.dot(left, right, preferred_element_type=jnp.float32)
+
+
 def start_reading(sources, raw, sems):
     copies = [
         pltpu.make_async_copy(source, raw.at[k], sems.at[k]) for k, source in enumerate(sources)
@@ -110,7 +119,7 @@
     return copies
 
 
-def filter_kernel(planes, halves, arriving, raw, terms, target_array, out, sems, y0, y1, y2, y3):
+def filter_kernel(planes, halves, arriving, raw, terms, target_array, out, sems, y0, y1, y2, y3, turn):
     for k in range(3):
         if k < len(arriving):
             arriving[k].wait()
@@ -123,6 +132,10 @@
     per_half = tiles // halves
     lane = lax.broadcasted_iota(jnp.int32, (CHUNK, LANES), 1)
     last, first = lane == LANES - 1, lane == 0
+    source_lane = lax.broadcasted_iota(jnp.int32, turn.shape, 0) % LANES
+    to = lax.broadcasted_iota(jnp.int32, turn.shape, 1)
+    wanted = lax.rem(to + jnp.where(to < LANES, 1, LANES - 1), LANES)
+    turn[...] = jnp.where(source_lane == wanted, 1.0, 0.0).astype(jnp.bfloat16)
     head, tail = lane < NZ, lane >= LANES - NZ
 
     def sweep(source, source_at, previous, previous_at, target, at, half_step):
@@ -135,6 +148,18 @@
 
             def tile(array, plane, t):
                 return array[plane, :, t * LANES : (t + 1) * LANES]
+
+            turned = dot(
+                jnp.concatenate(
+                    halved(jnp.concatenate([tile(source, s, t) for t in range(tiles)], axis=0)),
+                    axis=1,
+                ),
+                turn[...],
+            )
+
+            def moved(t, way):
+                t = t % tiles
+                return turned[CHUNK * t : CHUNK * (t + 1), way * LANES : (way + 1) * LANES]
 
             row = [tile(source, s, tiles - 1), tile(source, s, 0)]
             for t in range(tiles):
@@ -145,8 +170,8 @@
                 total = term[0] * here
                 total += term[1] * tile(source, s - 1, t)
                 total += term[2] * tile(source, s + 1, t)
-                total += term[3] * pltpu.roll(jnp.where(first, right, here), LANES - 1, 1)
-                total += term[4] * pltpu.roll(jnp.where(last, left, here), 1, 1)
+                total += term[3] * jnp.where(last, moved(t + 1, 0), moved(t, 0))
+                total += term[4] * jnp.where(first, moved(t - 1, 1), moved(t, 1))
                 total += term[5] * pltpu.roll(jnp.where(head, right, here), LANES - NZ, 1)
                 total += term[6] * pltpu.roll(jnp.where(tail, left, here), NZ, 1)
                 total = 0.5 * total if half_step else total - tile(previous, previous_at(w), t)
@@ -177,18 +202,20 @@
 
 
 def next_filter_kernel(
-    planes, halves, low, own, high, stored, target, raw, sems, out, y0, y1, y2, y3, terms
+    planes, halves, low, own, high, stored, target, raw, sems, out, y0, y1, y2, y3, terms, turn
 ):
     copies = start_reading((low, own, high), raw, sems)
     last = pltpu.make_async_copy(stored, terms, sems.at[3 + planes])
     last.start()
     filter_kernel(
-        planes, halves, (*copies, last), raw, terms, target, out, sems.at[pl.ds(3, planes)], y0, y1, y2, y3
+        planes, halves, (*copies, last), raw, terms, target, out, sems.at[pl.ds(3, planes)], y0, y1, y2, y3,
+        turn,
     )
 
 
 def first_filter_kernel(
-    planes, halves, scales, low, own, high, target, stored, raw, sems, out, y0, y1, y2, y3, terms, window
+    planes, halves, scales, low, own, high, target, stored, raw, sems, out, y0, y1, y2, y3, terms, turn,
+    window,
 ):
     for copy in start_reading((low, own, high), raw, sems):
         copy.wait()
@@ -196,7 +223,8 @@
     last = pltpu.make_async_copy(terms, stored, sems.at[3 + planes])
     last.start()
     filter_kernel(
-        planes, halves, (), raw, terms, target, out, sems.at[pl.ds(3, planes)], y0, y1, y2, y3
+        planes, halves, (), raw, terms, target, out, sems.at[pl.ds(3, planes)], y0, y1, y2, y3,
+        turn,
     )
     last.wait()
 
@@ -216,6 +244,7 @@
     scratch += [pltpu.VMEM((count, CHUNK, cells), jnp.float32) for count in steps]
     factors = jax.ShapeDtypeStruct((3 * planes - 2, 8, cells), jnp.float32)
     scratch.append(pltpu.VMEM(factors.shape, jnp.float32))
+    scratch.append(pltpu.VMEM((2 * LANES, 2 * LANES), jnp.bfloat16))
     options = dict(
         compiler_params=pltpu.CompilerParams(vmem_limit_bytes=60 * 2**20),
         cost_estimate=pl.CostEstimate(
@@ -248,15 +277,6 @@
 def rows_in_order(chunks):
     blocks = chunks[0].shape[0]
     return jnp.concatenate([c[b] for b in range(blocks) for c in chunks], axis=0)
-
-
-def halved(value):
-    high = value.astype(jnp.bfloat16)
-    return high, (value - high.astype(jnp.float32)).astype(jnp.bfloat16)
-
-
-def dot(left, right):
-    return jnp.dot(left, right, preferred_element_type=jnp.float32)
 
 
 def gram_kernel(*refs):
@@ -452,7 +472,7 @@
         low = lax.ppermute(own, "space", up)
         high = lax.ppermute(own, "space", back)
         if c >= 1:
-            low, high, part = lax.optimization_barrier((low, high, part))
+            low, high, _ = lax.optimization_barrier((low, high, part))
             if received:
                 part, received[-1] = lax.optimization_barrier((part, received[-1]))
             received.append(lax.all_to_all(part, "block", 0, 0, tiled=True))

time: 268 us -> 266 us (level)
  Pallas kernels: 87.4 us -> 83.1 us
    ppermute x4, waiting for transfers between devices: 13.2 us -> 16.5 us  [local(): low = lax.ppermute(own, 'space', up)]
    pallas_call x3, Pallas kernels: 42.6 us -> 39.4 us  [filtered(): pl.pallas_call(functools.partial(next_filter_kernel, planes, halves), out...]
  transfers between devices with their start and end apart: 11 -> 11, of which waited for: 7 -> 5; matrix products, arithmetic and copies ran while one was open for 1% -> 2% of each run, Pallas kernels for 23% -> 22%
where the time goes in v4:
time: 266 us
  blocking collectives  105 us (39%)
  Pallas kernels  83.1 us (31%)
  starting transfers between devices  37.7 us (14%)
  waiting for transfers between devices  31.2 us (12%)
  local copies, waits for them, and re-layouts  5.33 us (2%)
    all_to_all x1, blocking collectives, local(): sent = lax.all_to_all(result, 'block', 0, 0, tiled=True)  58.3 us
    pallas_call x3, Pallas kernels, filtered(): pl.pallas_call(functools.partial(next_filter_kernel, planes, halves), out...  39.4 us
    all_to_all x1, blocking collectives, local(): received.append(lax.all_to_all(part, 'block', 0, 0, tiled=True))  21 us
    ppermute x4, starting transfers between devices, local(): low = lax.ppermute(own, 'space', up)  20.8 us
    pallas_call x1, Pallas kernels, filtered(): pl.pallas_call(functools.partial(first_filter_kernel, planes, halves), ou...  18.1 us
    ppermute x4, waiting for transfers between devices, local(): low = lax.ppermute(own, 'space', up)  16.5 us
    ppermute x4, waiting for transfers between devices, local(): high = lax.ppermute(own, 'space', back)  14.7 us
    all_to_all x1, blocking collectives, local(): lax.all_to_all(pieces, ('space', 'block'), 0, 0, tiled=True)  13.2 us
  transfers between devices with their start and end apart: 11, of which 5 were waited for; matrix products, arithmetic and copies ran while one was open for 2% of the time, Pallas kernels for 22%

profile of v4, /device:TPU:0, one launch (start us, length us, event | category | flops | bytes accessed | tf_op | source)
XLA Modules:
  0.0 265.5 jit_solution(8254357372843137598)
XLA Ops:
  2.5 6.2 %collective-permute-start.2 = (f32[9,4,9216]{2,1,0:T(4,128)}, f32[9,4,9216]{2,1,0:T(4,128)}, u32[]{:S(2)}, u32[]{:S(2)}) collective-permute-start(f32[9,4,9216]{2,1,0:T(4,128)} %first_chunk.1.own), channel_id=1, source_target_pairs={{0,8},{8,16},{16,24},{1,9},{9,17},{17,25},{2,10},{10,18},{18,26},{... | collective-permute-start | bytes 3981320 | tf_op jit(solution)/shard_map/ppermute | solution.py:472
  10.1 3.3 %fusion = (f32[8,4,9216]{2,1,0:T(4,128)S(1)}, f32[8,4,9216]{2,1,0:T(4,128)S(1)}, f32[8,4,9216]{2,1,0:T(4,128)}) fusion(f32[32,4,9216]{2,1,0:T(4,128)} %vectors.1), kind=kLoop, calls=%fused_computation.1 | loop fusion | bytes 7077888 | tf_op jit(solution)/shard_map/slice | solution.py:471
  13.3 5.6 %collective-permute-start = (f32[8,4,9216]{2,1,0:T(4,128)S(1)}, f32[8,4,9216]{2,1,0:T(4,128)}, u32[]{:S(2)}, u32[]{:S(2)}) collective-permute-start(f32[8,4,9216]{2,1,0:T(4,128)S(1)} %get-tuple-element.34.own), channel_id=1, source_target_pairs={{0,8},{8,16},{16,24},{1,9},{9,17},{17,25},{2,10},{10,18},{18,26},{... | collective-permute-start | bytes 3538952 | tf_op jit(solution)/shard_map/ppermute | solution.py:472
  22.8 14.7 %collective-permute-done.2.low = f32[9,4,9216]{2,1,0:T(4,128)} collective-permute-done((f32[9,4,9216]{2,1,0:T(4,128)}, f32[9,4,9216]{2,1,0:T(4,128)}, u32[]{:S(2)}, u32[]{:S(2)}) %collective-permute-start.2) | collective-permute-done | bytes 1327136 | tf_op jit(solution)/shard_map/ppermute | solution.py:472
  37.4 5.6 %collective-permute-done.3.high = f32[9,4,9216]{2,1,0:T(4,128)} collective-permute-done((f32[9,4,9216]{2,1,0:T(4,128)}, f32[9,4,9216]{2,1,0:T(4,128)}, u32[]{:S(2)}, u32[]{:S(2)}) %collective-permute-start.3) | collective-permute-done | bytes 1327136 | tf_op jit(solution)/shard_map/ppermute | solution.py:473
  43.0 18.1 %first_chebyshev.1 = (f32[8,8,4608]{2,1,0:T(8,128)}, f32[10,8,9216]{2,1,0:T(8,128)}) custom-call(f32[2]{0:T(128)} %pad_maximum_fusion.scales, f32[9,4,9216]{2,1,0:T(4,128)} %collective-permute-done.2.low, f32[9,4,9216]{2,1,0:T(4,128)} %first_chunk.1.own, f32[9,4,9216]{2,1,0:T(4,128)} %collective-permute-done.3.high), custom_call_target="tpu_custom_call" | custom-call | flops 28901376 | bytes 12976128 | tf_op jit(solution)/shard_map/first_chebyshev/pallas_call | solution.py:266
  61.1 3.7 %all-to-all-start = ((f32[8,8,4608]{2,1,0:T(8,128)}), f32[8,8,4608]{2,1,0:T(8,128)S(1)}, u32[]{:S(2)}, u32[]{:S(2)}) async-start(f32[8,8,4608]{2,1,0:T(8,128)} %get-tuple-element.19), calls=%async_computation | async-start | bytes 2359296 | tf_op jit(solution)/shard_map/all_to_all | solution.py:478
  64.9 3.4 %collective-permute-start.4 = (f32[8,4,9216]{2,1,0:T(4,128)}, f32[8,4,9216]{2,1,0:T(4,128)}, u32[]{:S(2)}, u32[]{:S(2)}) collective-permute-start(f32[8,4,9216]{2,1,0:T(4,128)} %get-tuple-element.35.own), channel_id=1, source_target_pairs={{0,8},{8,16},{16,24},{1,9},{9,17},{17,25},{2,10},{10,18},{18,26},{... | collective-permute-start | bytes 3538952 | tf_op jit(solution)/shard_map/ppermute | solution.py:472
  69.6 13.2 %chebyshev.3 = f32[8,8,4608]{2,1,0:T(8,128)} custom-call(f32[8,4,9216]{2,1,0:T(4,128)} %collective-permute-done.low, f32[8,4,9216]{2,1,0:T(4,128)} %copy-done.4, f32[8,4,9216]{2,1,0:T(4,128)} %collective-permute-done.1.high, f32[10,8,9216]{2,1,0:T(8,128)} %get-tuple-element.22.stored), custom_call_target="tpu_custom_call" | custom-call | flops 28901376 | bytes 12976128 | tf_op jit(solution)/shard_map/chebyshev/pallas_call | solution.py:257
  83.8 4.2 %all-to-all-start.1 = ((f32[8,8,4608]{2,1,0:T(8,128)}), f32[8,8,4608]{2,1,0:T(8,128)S(1)}, u32[]{:S(2)}, u32[]{:S(2)}) async-start(f32[8,8,4608]{2,1,0:T(8,128)} %chebyshev.3), calls=%async_computation.1 | async-start | bytes 2359296 | tf_op jit(solution)/shard_map/all_to_all | solution.py:478
  88.0 5.6 %collective-permute-start.6 = (f32[8,4,9216]{2,1,0:T(4,128)S(1)}, f32[8,4,9216]{2,1,0:T(4,128)}, u32[]{:S(2)}, u32[]{:S(2)}) collective-permute-start(f32[8,4,9216]{2,1,0:T(4,128)S(1)} %get-tuple-element.33.own), channel_id=1, source_target_pairs={{0,8},{8,16},{16,24},{1,9},{9,17},{17,25},{2,10},{10,18},{18,26},{... | collective-permute-start | bytes 3538952 | tf_op jit(solution)/shard_map/ppermute | solution.py:472
  94.8 3.8 %collective-permute-done.5.high = f32[8,4,9216]{2,1,0:T(4,128)} collective-permute-done((f32[8,4,9216]{2,1,0:T(4,128)}, f32[8,4,9216]{2,1,0:T(4,128)}, u32[]{:S(2)}, u32[]{:S(2)}) %collective-permute-start.5) | collective-permute-done | bytes 1179680 | tf_op jit(solution)/shard_map/ppermute | solution.py:473
  98.7 13.1 %chebyshev.4 = f32[8,8,4608]{2,1,0:T(8,128)} custom-call(f32[8,4,9216]{2,1,0:T(4,128)} %collective-permute-done.4.low, f32[8,4,9216]{2,1,0:T(4,128)} %get-tuple-element.35.own, f32[8,4,9216]{2,1,0:T(4,128)} %collective-permute-done.5.high, f32[10,8,9216]{2,1,0:T(8,128)} %get-tuple-element.22.stored), custom_call_target="tpu_custom_call" | custom-call | flops 28901376 | bytes 12976128 | tf_op jit(solution)/shard_map/chebyshev/pallas_call | solution.py:257
  112.9 3.8 %all-to-all-start.2 = ((f32[8,8,4608]{2,1,0:T(8,128)}), f32[8,8,4608]{2,1,0:T(8,128)S(1)}, u32[]{:S(2)}, u32[]{:S(2)}) async-start(f32[8,8,4608]{2,1,0:T(8,128)} %chebyshev.4), calls=%async_computation.2 | async-start | bytes 2359296 | tf_op jit(solution)/shard_map/all_to_all | solution.py:478
  118.6 5.3 %collective-permute-done.7.high = f32[8,4,9216]{2,1,0:T(4,128)} collective-permute-done((f32[8,4,9216]{2,1,0:T(4,128)S(1)}, f32[8,4,9216]{2,1,0:T(4,128)}, u32[]{:S(2)}, u32[]{:S(2)}) %collective-permute-start.7) | collective-permute-done | bytes 1179680 | tf_op jit(solution)/shard_map/ppermute | solution.py:473
  123.8 13.1 %chebyshev.5 = f32[8,8,4608]{2,1,0:T(8,128)} custom-call(f32[8,4,9216]{2,1,0:T(4,128)} %collective-permute-done.6.low, f32[8,4,9216]{2,1,0:T(4,128)} %copy-done.3, f32[8,4,9216]{2,1,0:T(4,128)} %collective-permute-done.7.high, f32[10,8,9216]{2,1,0:T(8,128)} %get-tuple-element.22.stored), custom_call_target="tpu_custom_call" | custom-call | flops 28901376 | bytes 12976128 | tf_op jit(solution)/shard_map/chebyshev/pallas_call | solution.py:257
  137.0 21.0 %all_to_all.35.refs_3_ = f32[8,8,4608]{2,1,0:T(8,128)} all-to-all(f32[8,8,4608]{2,1,0:T(8,128)} %chebyshev.5), channel_id=1, replica_groups=mesh['space'=4,'block'=8] {'block'}, dimensions={0} | all-to-all | bytes 2359296 | tf_op jit(solution)/shard_map/all_to_all | solution.py:484
  158.0 4.2 %partial_gram.1 = f32[32,8,256]{2,1,0:T(8,128)} custom-call(f32[8,8,4608]{2,1,0:T(8,128)} %copy-done, f32[8,8,4608]{2,1,0:T(8,128)} %copy-done.1, f32[8,8,4608]{2,1,0:T(8,128)} %copy-done.2, f32[8,8,4608]{2,1,0:T(8,128)} %all_to_all.35.refs_3_), custom_call_target="tpu_custom_call" | custom-call | tf_op jit(solution)/shard_map/partial_gram/pallas_call | solution.py:315
  162.2 13.2 %all_to_all.36 = f32[32,8,256]{2,1,0:T(8,128)S(1)} all-to-all(f32[32,8,256]{2,1,0:T(8,128)} %partial_gram.1), channel_id=1, replica_groups=mesh['space'=4,'block'=8] {'space','block'}, dimensions={0} | all-to-all | bytes 524288 | tf_op jit(solution)/shard_map/all_to_all | solution.py:487
  175.4 13.0 %all_to_all.37 = f32[32,8,256]{2,1,0:T(8,128)} all-to-all(f32[32,8,256]{2,1,0:T(8,128)S(1)} %broadcast_in_dim.2), channel_id=1, replica_groups=mesh['space'=4,'block'=8] {'space','block'}, dimensions={0} | all-to-all | bytes 524288 | tf_op jit(solution)/shard_map/all_to_all | solution.py:488
  188.4 10.2 %inverse_factor.1.inverse = f32[256,256]{1,0:T(8,128)} custom-call(f32[256,256]{1,0:T(8,128)} %bitcast.5), custom_call_target="tpu_custom_call" | custom-call | tf_op jit(solution)/shard_map/inverse_factor/pallas_call | solution.py:440
  198.6 5.7 %product.1 = f32[8,32,4608]{2,1,0:T(8,128)} custom-call(f32[256,256]{1,0:T(8,128)} %inverse_factor.1.inverse, f32[8,8,4608]{2,1,0:T(8,128)} %copy-done, f32[8,8,4608]{2,1,0:T(8,128)} %copy-done.1, f32[8,8,4608]{2,1,0:T(8,128)} %copy-done.2, f32[8,8,4608]{2,1,0:T(8,128)} %all_to_all.35.refs_3_), custom_call_target="tpu_custom_call" | custom-call | tf_op jit(solution)/shard_map/product/pallas_call | solution.py:336
  204.3 58.3 %all_to_all.38 = f32[8,32,4608]{2,1,0:T(8,128)S(1)} all-to-all(f32[8,32,4608]{2,1,0:T(8,128)} %product.1), channel_id=1, replica_groups=mesh['space'=4,'block'=8] {'block'}, dimensions={0} | all-to-all | bytes 9437184 | tf_op jit(solution)/shard_map/all_to_all | solution.py:493
  262.6 3.0 %assemble.1 = f32[32,4,9216]{2,1,0:T(4,128)} custom-call(f32[4,2,32,4608]{3,2,1,0:T(8,128)S(1)} %bitcast.4), custom_call_target="tpu_custom_call" | custom-call | tf_op jit(solution)/shard_map/assemble/pallas_call | solution.py:356
  (28 shorter events, 12.9 us)
Async XLA Ops:
  2.5 17.6 %copy-start.5 = (f32[3]{0:T(128)S(1)}, f32[3]{0:T(128)}, u32[]{:S(2)}) copy-start(f32[3]{0:T(128)} %table.1) | copy-start | bytes 40
  2.5 34.9 %collective-permute-start.2 = (f32[9,4,9216]{2,1,0:T(4,128)}, f32[9,4,9216]{2,1,0:T(4,128)}, u32[]{:S(2)}, u32[]{:S(2)}) collective-permute-start(f32[9,4,9216]{2,1,0:T(4,128)} %first_chunk.1.own), channel_id=1, source_target_pairs={{0,8},{8,16},{16,24},{1,9},{9,17},{17,25},{2,10},{10,18},{18,26},{... | collective-permute-start | bytes 3981320 | tf_op jit(solution)/shard_map/ppermute | solution.py:472
  8.8 34.3 %collective-permute-start.3 = (f32[9,4,9216]{2,1,0:T(4,128)}, f32[9,4,9216]{2,1,0:T(4,128)}, u32[]{:S(2)}, u32[]{:S(2)}) collective-permute-start(f32[9,4,9216]{2,1,0:T(4,128)} %first_chunk.1.own), channel_id=1, source_target_pairs={{8,0},{16,8},{24,16},{9,1},{17,9},{25,17},{10,2},{18,10},{26,18},{... | collective-permute-start | bytes 3981320 | tf_op jit(solution)/shard_map/ppermute | solution.py:473
  13.3 47.8 %copy-start.4 = (f32[8,4,9216]{2,1,0:T(4,128)}, f32[8,4,9216]{2,1,0:T(4,128)S(1)}, u32[]{:S(2)}) copy-start(f32[8,4,9216]{2,1,0:T(4,128)S(1)} %get-tuple-element.34.own) | copy-start | bytes 3538948
  13.3 80.2 %copy-start.3 = (f32[8,4,9216]{2,1,0:T(4,128)}, f32[8,4,9216]{2,1,0:T(4,128)S(1)}, u32[]{:S(2)}) copy-start(f32[8,4,9216]{2,1,0:T(4,128)S(1)} %get-tuple-element.33.own) | copy-start | bytes 3538948
  13.3 56.2 %collective-permute-start = (f32[8,4,9216]{2,1,0:T(4,128)S(1)}, f32[8,4,9216]{2,1,0:T(4,128)}, u32[]{:S(2)}, u32[]{:S(2)}) collective-permute-start(f32[8,4,9216]{2,1,0:T(4,128)S(1)} %get-tuple-element.34.own), channel_id=1, source_target_pairs={{0,8},{8,16},{16,24},{1,9},{9,17},{17,25},{2,10},{10,18},{18,26},{... | collective-permute-start | bytes 3538952 | tf_op jit(solution)/shard_map/ppermute | solution.py:472
  18.9 50.7 %collective-permute-start.1 = (f32[8,4,9216]{2,1,0:T(4,128)S(1)}, f32[8,4,9216]{2,1,0:T(4,128)}, u32[]{:S(2)}, u32[]{:S(2)}) collective-permute-start(f32[8,4,9216]{2,1,0:T(4,128)S(1)} %get-tuple-element.34.own), channel_id=1, source_target_pairs={{8,0},{16,8},{24,16},{9,1},{17,9},{25,17},{10,2},{18,10},{26,18},{... | collective-permute-start | bytes 3538952 | tf_op jit(solution)/shard_map/ppermute | solution.py:473
  61.1 21.6 %all-to-all-start = ((f32[8,8,4608]{2,1,0:T(8,128)}), f32[8,8,4608]{2,1,0:T(8,128)S(1)}, u32[]{:S(2)}, u32[]{:S(2)}) async-start(f32[8,8,4608]{2,1,0:T(8,128)} %get-tuple-element.19), calls=%async_computation | async-start | bytes 2359296 | tf_op jit(solution)/shard_map/all_to_all | solution.py:478
  64.9 30.0 %collective-permute-start.4 = (f32[8,4,9216]{2,1,0:T(4,128)}, f32[8,4,9216]{2,1,0:T(4,128)}, u32[]{:S(2)}, u32[]{:S(2)}) collective-permute-start(f32[8,4,9216]{2,1,0:T(4,128)} %get-tuple-element.35.own), channel_id=1, source_target_pairs={{0,8},{8,16},{16,24},{1,9},{9,17},{17,25},{2,10},{10,18},{18,26},{... | collective-permute-start | bytes 3538952 | tf_op jit(solution)/shard_map/ppermute | solution.py:472
  68.2 30.4 %collective-permute-start.5 = (f32[8,4,9216]{2,1,0:T(4,128)}, f32[8,4,9216]{2,1,0:T(4,128)}, u32[]{:S(2)}, u32[]{:S(2)}) collective-permute-start(f32[8,4,9216]{2,1,0:T(4,128)} %get-tuple-element.35.own), channel_id=1, source_target_pairs={{8,0},{16,8},{24,16},{9,1},{17,9},{25,17},{10,2},{18,10},{26,18},{... | collective-permute-start | bytes 3538952 | tf_op jit(solution)/shard_map/ppermute | solution.py:473
  82.7 1.0 copy-start
  83.8 28.1 %all-to-all-start.1 = ((f32[8,8,4608]{2,1,0:T(8,128)}), f32[8,8,4608]{2,1,0:T(8,128)S(1)}, u32[]{:S(2)}, u32[]{:S(2)}) async-start(f32[8,8,4608]{2,1,0:T(8,128)} %chebyshev.3), calls=%async_computation.1 | async-start | bytes 2359296 | tf_op jit(solution)/shard_map/all_to_all | solution.py:478
  88.0 30.6 %collective-permute-start.6 = (f32[8,4,9216]{2,1,0:T(4,128)S(1)}, f32[8,4,9216]{2,1,0:T(4,128)}, u32[]{:S(2)}, u32[]{:S(2)}) collective-permute-start(f32[8,4,9216]{2,1,0:T(4,128)S(1)} %get-tuple-element.33.own), channel_id=1, source_target_pairs={{0,8},{8,16},{16,24},{1,9},{9,17},{17,25},{2,10},{10,18},{18,26},{... | collective-permute-start | bytes 3538952 | tf_op jit(solution)/shard_map/ppermute | solution.py:472
  93.5 30.3 %collective-permute-start.7 = (f32[8,4,9216]{2,1,0:T(4,128)S(1)}, f32[8,4,9216]{2,1,0:T(4,128)}, u32[]{:S(2)}, u32[]{:S(2)}) collective-permute-start(f32[8,4,9216]{2,1,0:T(4,128)S(1)} %get-tuple-element.33.own), channel_id=1, source_target_pairs={{8,0},{16,8},{24,16},{9,1},{17,9},{25,17},{10,2},{18,10},{26,18},{... | collective-permute-start | bytes 3538952 | tf_op jit(solution)/shard_map/ppermute | solution.py:473
  111.8 1.0 copy-start.1
  112.9 24.1 %all-to-all-start.2 = ((f32[8,8,4608]{2,1,0:T(8,128)}), f32[8,8,4608]{2,1,0:T(8,128)S(1)}, u32[]{:S(2)}, u32[]{:S(2)}) async-start(f32[8,8,4608]{2,1,0:T(8,128)} %chebyshev.4), calls=%async_computation.2 | async-start | bytes 2359296 | tf_op jit(solution)/shard_map/all_to_all | solution.py:478
  137.0 21.0 %copy-start.2 = (f32[8,8,4608]{2,1,0:T(8,128)}, f32[8,8,4608]{2,1,0:T(8,128)S(1)}, u32[]{:S(2)}) copy-start(f32[8,8,4608]{2,1,0:T(8,128)S(1)} %all-to-all-done.2.refs_2_) | copy-start | bytes 3538948

commit v5 on v4

--- a/solution.py
+++ b/solution.py
@@ -340,7 +340,7 @@
         in_specs=[pl.BlockSpec((rank, rank), lambda i: (0, 0))]
         + [pl.BlockSpec((blocks, rows, BLOCK), lambda i: (0, 0, i))] * len(chunks),
         out_specs=pl.BlockSpec((blocks, rank // blocks, BLOCK), lambda i: (0, 0, i)),
-        compiler_params=pltpu.CompilerParams(vmem_limit_bytes=60 * 2**20),
+        compiler_params=pltpu.CompilerParams(vmem_limit_bytes=32 * 2**20),
         name="product",
     )(inverse, *chunks)
 

time: 266 us -> 266 us (level)
  local copies, waits for them, and re-layouts: 5.33 us -> 8.86 us
  Pallas kernels: 83.1 us -> 80.4 us
    unnamed x12 -> x22, local copies, waits for them, and re-layouts: 2.05 us -> 5.56 us
    pallas_call x1, Pallas kernels: 5.65 us -> 2.86 us  [product(): pl.pallas_call(product_kernel, grid=(width // BLOCK,), out_shape=jax.Shap...]
where the time goes in v5:
time: 266 us; the launch traced here: 265 us
  blocking collectives  105 us (39%)
  Pallas kernels  80.4 us (30%)
  starting transfers between devices  37.7 us (14%)
  waiting for transfers between devices  31.2 us (12%)
  local copies, waits for them, and re-layouts  8.86 us (3%)
    all_to_all x1, blocking collectives, local(): sent = lax.all_to_all(result, 'block', 0, 0, tiled=True)  57.2 us
    pallas_call x3, Pallas kernels, filtered(): pl.pallas_call(functools.partial(next_filter_kernel, planes, halves), out...  39.4 us
    all_to_all x1, blocking collectives, local(): received.append(lax.all_to_all(part, 'block', 0, 0, tiled=True))  21 us
    ppermute x4, starting transfers between devices, local(): low = lax.ppermute(own, 'space', up)  20.8 us
    pallas_call x1, Pallas kernels, filtered(): pl.pallas_call(functools.partial(first_filter_kernel, planes, halves), ou...  18.1 us
    ppermute x4, waiting for transfers between devices, local(): low = lax.ppermute(own, 'space', up)  16.9 us
    ppermute x4, waiting for transfers between devices, local(): high = lax.ppermute(own, 'space', back)  14.2 us
    all_to_all x1, blocking collectives, local(): lax.all_to_all(pieces, ('space', 'block'), 0, 0, tiled=True)  13.3 us
  transfers between devices with their start and end apart: 11, of which 5 were waited for; matrix products, arithmetic and copies ran while one was open for 2% of the time, Pallas kernels for 22%

profile of v5, /device:TPU:0, one launch (start us, length us, event | category | flops | bytes accessed | tf_op | source)
XLA Modules:
  0.0 265.4 jit_solution(2728008899296953955)
XLA Ops:
  2.6 6.2 %collective-permute-start.2 = (f32[9,4,9216]{2,1,0:T(4,128)}, f32[9,4,9216]{2,1,0:T(4,128)}, u32[]{:S(2)}, u32[]{:S(2)}) collective-permute-start(f32[9,4,9216]{2,1,0:T(4,128)} %first_chunk.1.own), channel_id=1, source_target_pairs={{0,8},{8,16},{16,24},{1,9},{9,17},{17,25},{2,10},{10,18},{18,26},{... | collective-permute-start | bytes 3981320 | tf_op jit(solution)/shard_map/ppermute | solution.py:472
  10.1 3.3 %fusion = (f32[8,4,9216]{2,1,0:T(4,128)}, f32[8,4,9216]{2,1,0:T(4,128)S(1)}, f32[8,4,9216]{2,1,0:T(4,128)S(1)}) fusion(f32[32,4,9216]{2,1,0:T(4,128)} %vectors.1), kind=kLoop, calls=%fused_computation.1 | loop fusion | bytes 7077888 | tf_op jit(solution)/shard_map/slice | solution.py:471
  13.4 5.6 %collective-permute-start = (f32[8,4,9216]{2,1,0:T(4,128)S(1)}, f32[8,4,9216]{2,1,0:T(4,128)}, u32[]{:S(2)}, u32[]{:S(2)}) collective-permute-start(f32[8,4,9216]{2,1,0:T(4,128)S(1)} %get-tuple-element.34.own), channel_id=1, source_target_pairs={{0,8},{8,16},{16,24},{1,9},{9,17},{17,25},{2,10},{10,18},{18,26},{... | collective-permute-start | bytes 3538952 | tf_op jit(solution)/shard_map/ppermute | solution.py:472
  22.8 14.7 %collective-permute-done.2.low = f32[9,4,9216]{2,1,0:T(4,128)} collective-permute-done((f32[9,4,9216]{2,1,0:T(4,128)}, f32[9,4,9216]{2,1,0:T(4,128)}, u32[]{:S(2)}, u32[]{:S(2)}) %collective-permute-start.2) | collective-permute-done | bytes 1327136 | tf_op jit(solution)/shard_map/ppermute | solution.py:472
  37.5 5.6 %collective-permute-done.3.high = f32[9,4,9216]{2,1,0:T(4,128)} collective-permute-done((f32[9,4,9216]{2,1,0:T(4,128)}, f32[9,4,9216]{2,1,0:T(4,128)}, u32[]{:S(2)}, u32[]{:S(2)}) %collective-permute-start.3) | collective-permute-done | bytes 1327136 | tf_op jit(solution)/shard_map/ppermute | solution.py:473
  43.0 18.1 %first_chebyshev.1 = (f32[8,8,4608]{2,1,0:T(8,128)}, f32[10,8,9216]{2,1,0:T(8,128)}) custom-call(f32[2]{0:T(128)} %pad_maximum_fusion.scales, f32[9,4,9216]{2,1,0:T(4,128)} %collective-permute-done.2.low, f32[9,4,9216]{2,1,0:T(4,128)} %first_chunk.1.own, f32[9,4,9216]{2,1,0:T(4,128)} %collective-permute-done.3.high), custom_call_target="tpu_custom_call" | custom-call | flops 28901376 | bytes 12976128 | tf_op jit(solution)/shard_map/first_chebyshev/pallas_call | solution.py:266
  61.2 3.7 %all-to-all-start = ((f32[8,8,4608]{2,1,0:T(8,128)}), f32[8,8,4608]{2,1,0:T(8,128)S(1)}, u32[]{:S(2)}, u32[]{:S(2)}) async-start(f32[8,8,4608]{2,1,0:T(8,128)} %get-tuple-element.19), calls=%async_computation | async-start | bytes 2359296 | tf_op jit(solution)/shard_map/all_to_all | solution.py:478
  64.9 3.4 %collective-permute-start.4 = (f32[8,4,9216]{2,1,0:T(4,128)S(1)}, f32[8,4,9216]{2,1,0:T(4,128)}, u32[]{:S(2)}, u32[]{:S(2)}) collective-permute-start(f32[8,4,9216]{2,1,0:T(4,128)S(1)} %get-tuple-element.35.own), channel_id=1, source_target_pairs={{0,8},{8,16},{16,24},{1,9},{9,17},{17,25},{2,10},{10,18},{18,26},{... | collective-permute-start | bytes 3538952 | tf_op jit(solution)/shard_map/ppermute | solution.py:472
  69.6 13.1 %chebyshev.3 = f32[8,8,4608]{2,1,0:T(8,128)} custom-call(f32[8,4,9216]{2,1,0:T(4,128)} %collective-permute-done.low, f32[8,4,9216]{2,1,0:T(4,128)} %copy-done.9, f32[8,4,9216]{2,1,0:T(4,128)} %collective-permute-done.1.high, f32[10,8,9216]{2,1,0:T(8,128)} %get-tuple-element.22.stored), custom_call_target="tpu_custom_call" | custom-call | flops 28901376 | bytes 12976128 | tf_op jit(solution)/shard_map/chebyshev/pallas_call | solution.py:257
  83.8 4.2 %all-to-all-start.1 = ((f32[8,8,4608]{2,1,0:T(8,128)}), f32[8,8,4608]{2,1,0:T(8,128)S(1)}, u32[]{:S(2)}, u32[]{:S(2)}) async-start(f32[8,8,4608]{2,1,0:T(8,128)} %chebyshev.3), calls=%async_computation.1 | async-start | bytes 2359296 | tf_op jit(solution)/shard_map/all_to_all | solution.py:478
  88.0 5.6 %collective-permute-start.6 = (f32[8,4,9216]{2,1,0:T(4,128)}, f32[8,4,9216]{2,1,0:T(4,128)}, u32[]{:S(2)}, u32[]{:S(2)}) collective-permute-start(f32[8,4,9216]{2,1,0:T(4,128)} %get-tuple-element.33.own), channel_id=1, source_target_pairs={{0,8},{8,16},{16,24},{1,9},{9,17},{17,25},{2,10},{10,18},{18,26},{... | collective-permute-start | bytes 3538952 | tf_op jit(solution)/shard_map/ppermute | solution.py:472
  94.9 3.5 %collective-permute-done.5.high = f32[8,4,9216]{2,1,0:T(4,128)} collective-permute-done((f32[8,4,9216]{2,1,0:T(4,128)S(1)}, f32[8,4,9216]{2,1,0:T(4,128)}, u32[]{:S(2)}, u32[]{:S(2)}) %collective-permute-start.5) | collective-permute-done | bytes 1179680 | tf_op jit(solution)/shard_map/ppermute | solution.py:473
  98.4 13.1 %chebyshev.4 = f32[8,8,4608]{2,1,0:T(8,128)} custom-call(f32[8,4,9216]{2,1,0:T(4,128)} %collective-permute-done.4.low, f32[8,4,9216]{2,1,0:T(4,128)} %copy-done.8, f32[8,4,9216]{2,1,0:T(4,128)} %collective-permute-done.5.high, f32[10,8,9216]{2,1,0:T(8,128)} %get-tuple-element.22.stored), custom_call_target="tpu_custom_call" | custom-call | flops 28901376 | bytes 12976128 | tf_op jit(solution)/shard_map/chebyshev/pallas_call | solution.py:257
  112.6 3.9 %all-to-all-start.2 = ((f32[8,8,4608]{2,1,0:T(8,128)}), f32[8,8,4608]{2,1,0:T(8,128)S(1)}, u32[]{:S(2)}, u32[]{:S(2)}) async-start(f32[8,8,4608]{2,1,0:T(8,128)} %chebyshev.4), calls=%async_computation.2 | async-start | bytes 2359296 | tf_op jit(solution)/shard_map/all_to_all | solution.py:478
  118.7 5.2 %collective-permute-done.7.high = f32[8,4,9216]{2,1,0:T(4,128)} collective-permute-done((f32[8,4,9216]{2,1,0:T(4,128)}, f32[8,4,9216]{2,1,0:T(4,128)}, u32[]{:S(2)}, u32[]{:S(2)}) %collective-permute-start.7) | collective-permute-done | bytes 1179680 | tf_op jit(solution)/shard_map/ppermute | solution.py:473
  123.9 13.1 %chebyshev.5 = f32[8,8,4608]{2,1,0:T(8,128)} custom-call(f32[8,4,9216]{2,1,0:T(4,128)} %collective-permute-done.6.low, f32[8,4,9216]{2,1,0:T(4,128)} %get-tuple-element.33.own, f32[8,4,9216]{2,1,0:T(4,128)} %collective-permute-done.7.high, f32[10,8,9216]{2,1,0:T(8,128)} %get-tuple-element.22.stored), custom_call_target="tpu_custom_call" | custom-call | flops 28901376 | bytes 12976128 | tf_op jit(solution)/shard_map/chebyshev/pallas_call | solution.py:257
  137.0 21.0 %all_to_all.35.refs_3_ = f32[8,8,4608]{2,1,0:T(8,128)} all-to-all(f32[8,8,4608]{2,1,0:T(8,128)} %chebyshev.5), channel_id=1, replica_groups=mesh['space'=4,'block'=8] {'block'}, dimensions={0} | all-to-all | bytes 2359296 | tf_op jit(solution)/shard_map/all_to_all | solution.py:484
  158.1 4.3 %partial_gram.1 = f32[32,8,256]{2,1,0:T(8,128)} custom-call(f32[8,8,4608]{2,1,0:T(8,128)} %copy-done, f32[8,8,4608]{2,1,0:T(8,128)} %copy-done.2, f32[8,8,4608]{2,1,0:T(8,128)} %copy-done.4, f32[8,8,4608]{2,1,0:T(8,128)} %all_to_all.35.refs_3_), custom_call_target="tpu_custom_call" | custom-call | tf_op jit(solution)/shard_map/partial_gram/pallas_call | solution.py:315
  162.3 13.3 %all_to_all.36 = f32[32,8,256]{2,1,0:T(8,128)S(1)} all-to-all(f32[32,8,256]{2,1,0:T(8,128)} %partial_gram.1), channel_id=1, replica_groups=mesh['space'=4,'block'=8] {'space','block'}, dimensions={0} | all-to-all | bytes 524288 | tf_op jit(solution)/shard_map/all_to_all | solution.py:487
  175.7 13.0 %all_to_all.37 = f32[32,8,256]{2,1,0:T(8,128)} all-to-all(f32[32,8,256]{2,1,0:T(8,128)S(1)} %broadcast_in_dim.2), channel_id=1, replica_groups=mesh['space'=4,'block'=8] {'space','block'}, dimensions={0} | all-to-all | bytes 524288 | tf_op jit(solution)/shard_map/all_to_all | solution.py:488
  188.7 10.2 %inverse_factor.1.inverse = f32[256,256]{1,0:T(8,128)} custom-call(f32[256,256]{1,0:T(8,128)} %bitcast.5), custom_call_target="tpu_custom_call" | custom-call | tf_op jit(solution)/shard_map/inverse_factor/pallas_call | solution.py:440
  202.4 2.9 %product.1 = f32[8,32,4608]{2,1,0:T(8,128)S(1)} custom-call(f32[256,256]{1,0:T(8,128)S(1)} %copy-done.7, f32[8,8,4608]{2,1,0:T(8,128)S(1)} %copy-done.1, f32[8,8,4608]{2,1,0:T(8,128)S(1)} %copy-done.3, f32[8,8,4608]{2,1,0:T(8,128)S(1)} %copy-done.5, f32[8,8,4608]{2,1,0:T(8,128)S(1)} %copy-done.6), custom_call_target="tpu_custom_call" | custom-call | tf_op jit(solution)/shard_map/product/pallas_call | solution.py:336
  205.3 57.2 %all_to_all.38 = f32[8,32,4608]{2,1,0:T(8,128)S(1)} all-to-all(f32[8,32,4608]{2,1,0:T(8,128)S(1)} %product.1), channel_id=1, replica_groups=mesh['space'=4,'block'=8] {'block'}, dimensions={0} | all-to-all | bytes 9437184 | tf_op jit(solution)/shard_map/all_to_all | solution.py:493
  262.5 3.0 %assemble.1 = f32[32,4,9216]{2,1,0:T(4,128)} custom-call(f32[4,2,32,4608]{3,2,1,0:T(8,128)S(1)} %bitcast.4), custom_call_target="tpu_custom_call" | custom-call | tf_op jit(solution)/shard_map/assemble/pallas_call | solution.py:356
  (38 shorter events, 16.8 us)
Async XLA Ops:
  2.6 17.7 %copy-start.10 = (f32[3]{0:T(128)S(1)}, f32[3]{0:T(128)}, u32[]{:S(2)}) copy-start(f32[3]{0:T(128)} %table.1) | copy-start | bytes 40
  2.6 34.9 %collective-permute-start.2 = (f32[9,4,9216]{2,1,0:T(4,128)}, f32[9,4,9216]{2,1,0:T(4,128)}, u32[]{:S(2)}, u32[]{:S(2)}) collective-permute-start(f32[9,4,9216]{2,1,0:T(4,128)} %first_chunk.1.own), channel_id=1, source_target_pairs={{0,8},{8,16},{16,24},{1,9},{9,17},{17,25},{2,10},{10,18},{18,26},{... | collective-permute-start | bytes 3981320 | tf_op jit(solution)/shard_map/ppermute | solution.py:472
  8.8 34.3 %collective-permute-start.3 = (f32[9,4,9216]{2,1,0:T(4,128)}, f32[9,4,9216]{2,1,0:T(4,128)}, u32[]{:S(2)}, u32[]{:S(2)}) collective-permute-start(f32[9,4,9216]{2,1,0:T(4,128)} %first_chunk.1.own), channel_id=1, source_target_pairs={{8,0},{16,8},{24,16},{9,1},{17,9},{25,17},{10,2},{18,10},{26,18},{... | collective-permute-start | bytes 3981320 | tf_op jit(solution)/shard_map/ppermute | solution.py:473
  13.4 47.8 %copy-start.9 = (f32[8,4,9216]{2,1,0:T(4,128)}, f32[8,4,9216]{2,1,0:T(4,128)S(1)}, u32[]{:S(2)}) copy-start(f32[8,4,9216]{2,1,0:T(4,128)S(1)} %get-tuple-element.34.own) | copy-start | bytes 3538948
  13.4 54.9 %copy-start.8 = (f32[8,4,9216]{2,1,0:T(4,128)}, f32[8,4,9216]{2,1,0:T(4,128)S(1)}, u32[]{:S(2)}) copy-start(f32[8,4,9216]{2,1,0:T(4,128)S(1)} %get-tuple-element.35.own) | copy-start | bytes 3538948
  13.4 56.2 %collective-permute-start = (f32[8,4,9216]{2,1,0:T(4,128)S(1)}, f32[8,4,9216]{2,1,0:T(4,128)}, u32[]{:S(2)}, u32[]{:S(2)}) collective-permute-start(f32[8,4,9216]{2,1,0:T(4,128)S(1)} %get-tuple-element.34.own), channel_id=1, source_target_pairs={{0,8},{8,16},{16,24},{1,9},{9,17},{17,25},{2,10},{10,18},{18,26},{... | collective-permute-start | bytes 3538952 | tf_op jit(solution)/shard_map/ppermute | solution.py:472
  18.9 50.6 %collective-permute-start.1 = (f32[8,4,9216]{2,1,0:T(4,128)S(1)}, f32[8,4,9216]{2,1,0:T(4,128)}, u32[]{:S(2)}, u32[]{:S(2)}) collective-permute-start(f32[8,4,9216]{2,1,0:T(4,128)S(1)} %get-tuple-element.34.own), channel_id=1, source_target_pairs={{8,0},{16,8},{24,16},{9,1},{17,9},{25,17},{10,2},{18,10},{26,18},{... | collective-permute-start | bytes 3538952 | tf_op jit(solution)/shard_map/ppermute | solution.py:473
  61.2 21.6 %all-to-all-start = ((f32[8,8,4608]{2,1,0:T(8,128)}), f32[8,8,4608]{2,1,0:T(8,128)S(1)}, u32[]{:S(2)}, u32[]{:S(2)}) async-start(f32[8,8,4608]{2,1,0:T(8,128)} %get-tuple-element.19), calls=%async_computation | async-start | bytes 2359296 | tf_op jit(solution)/shard_map/all_to_all | solution.py:478
  64.9 30.0 %collective-permute-start.4 = (f32[8,4,9216]{2,1,0:T(4,128)S(1)}, f32[8,4,9216]{2,1,0:T(4,128)}, u32[]{:S(2)}, u32[]{:S(2)}) collective-permute-start(f32[8,4,9216]{2,1,0:T(4,128)S(1)} %get-tuple-element.35.own), channel_id=1, source_target_pairs={{0,8},{8,16},{16,24},{1,9},{9,17},{17,25},{2,10},{10,18},{18,26},{... | collective-permute-start | bytes 3538952 | tf_op jit(solution)/shard_map/ppermute | solution.py:472
  68.3 30.1 %collective-permute-start.5 = (f32[8,4,9216]{2,1,0:T(4,128)S(1)}, f32[8,4,9216]{2,1,0:T(4,128)}, u32[]{:S(2)}, u32[]{:S(2)}) collective-permute-start(f32[8,4,9216]{2,1,0:T(4,128)S(1)} %get-tuple-element.35.own), channel_id=1, source_target_pairs={{8,0},{16,8},{24,16},{9,1},{17,9},{25,17},{10,2},{18,10},{26,18},{... | collective-permute-start | bytes 3538952 | tf_op jit(solution)/shard_map/ppermute | solution.py:473
  82.8 1.0 copy-start
  83.8 27.8 %all-to-all-start.1 = ((f32[8,8,4608]{2,1,0:T(8,128)}), f32[8,8,4608]{2,1,0:T(8,128)S(1)}, u32[]{:S(2)}, u32[]{:S(2)}) async-start(f32[8,8,4608]{2,1,0:T(8,128)} %chebyshev.3), calls=%async_computation.1 | async-start | bytes 2359296 | tf_op jit(solution)/shard_map/all_to_all | solution.py:478
  88.0 30.7 %collective-permute-start.6 = (f32[8,4,9216]{2,1,0:T(4,128)}, f32[8,4,9216]{2,1,0:T(4,128)}, u32[]{:S(2)}, u32[]{:S(2)}) collective-permute-start(f32[8,4,9216]{2,1,0:T(4,128)} %get-tuple-element.33.own), channel_id=1, source_target_pairs={{0,8},{8,16},{16,24},{1,9},{9,17},{17,25},{2,10},{10,18},{18,26},{... | collective-permute-start | bytes 3538952 | tf_op jit(solution)/shard_map/ppermute | solution.py:472
  93.6 30.3 %collective-permute-start.7 = (f32[8,4,9216]{2,1,0:T(4,128)}, f32[8,4,9216]{2,1,0:T(4,128)}, u32[]{:S(2)}, u32[]{:S(2)}) collective-permute-start(f32[8,4,9216]{2,1,0:T(4,128)} %get-tuple-element.33.own), channel_id=1, source_target_pairs={{8,0},{16,8},{24,16},{9,1},{17,9},{25,17},{10,2},{18,10},{26,18},{... | collective-permute-start | bytes 3538952 | tf_op jit(solution)/shard_map/ppermute | solution.py:473
  111.5 1.1 copy-start.2
  112.6 24.4 %all-to-all-start.2 = ((f32[8,8,4608]{2,1,0:T(8,128)}), f32[8,8,4608]{2,1,0:T(8,128)S(1)}, u32[]{:S(2)}, u32[]{:S(2)}) async-start(f32[8,8,4608]{2,1,0:T(8,128)} %chebyshev.4), calls=%async_computation.2 | async-start | bytes 2359296 | tf_op jit(solution)/shard_map/all_to_all | solution.py:478
  137.0 21.0 %copy-start.4 = (f32[8,8,4608]{2,1,0:T(8,128)}, f32[8,8,4608]{2,1,0:T(8,128)S(1)}, u32[]{:S(2)}) copy-start(f32[8,8,4608]{2,1,0:T(8,128)S(1)} %all-to-all-done.2.refs_2_) | copy-start | bytes 3538948
  158.1 40.8 %copy-start.3 = (f32[8,8,4608]{2,1,0:T(8,128)S(1)}, f32[8,8,4608]{2,1,0:T(8,128)}, u32[]{:S(2)}) copy-start(f32[8,8,4608]{2,1,0:T(8,128)} %copy-done.2) | copy-start | bytes 3538948
  162.3 36.6 %copy-start.1 = (f32[8,8,4608]{2,1,0:T(8,128)S(1)}, f32[8,8,4608]{2,1,0:T(8,128)}, u32[]{:S(2)}) copy-start(f32[8,8,4608]{2,1,0:T(8,128)} %copy-done) | copy-start | bytes 3538948
  198.9 1.3 copy-start.5
  200.2 1.3 copy-start.6
  201.5 0.9 copy-start.7
